TPU v7x, 32 devices: a whole 2x2x4 slice. The times are simulated.
32 devices in a mesh: blk: 8 (over y, x, core), win: 4 (over z).
Axes of the slice: x: 2, y: 2, z: 4, core: 2. Of those that a mesh axis runs over, the one named last changes fastest.
Arguments:
- record: bfloat16 [4096, 4096], P('blk', 'win'), may hold values from -6 to 6
- deck_ids: int32 [32], replicated, may hold values from 0 to 1, as said below
- partners: int32 [32, 4], replicated, may hold values from 0 to 31, as said below
Outputs:
- correlations: bfloat16 [128, 64, 16384], P(('blk', 'win'))
Inputs may be any that keep to these rules, and one draw needn't show every extreme that they name: `deck_ids`: 0 on the first deck and 1 on the second; non-decreasing in the block id (a single switch from 0 to 1), and both decks occur. Row b lists the partner blocks of block b. Take the blocks in groups of 4 consecutive ids: the partners of the blocks of one group are all different, and they name exactly 2 blocks of every group.
All inputs are finite; a program needn't handle non-finite values.
Results may differ from a plain program's by a relative error of at most 0.0075.
Values may be sent and summed in bfloat16 or wider, within the bound.
A program may use at most 128 MiB of HBM per device.

v0:
```python
import math

import jax
import jax.numpy as jnp
from jax import lax
from jax.sharding import PartitionSpec as P

WS = 512
BINS = 128
LAGS = 64


def forward_table():
    samples = jnp.arange(WS, dtype=jnp.int32)
    frequency = jnp.arange(1, BINS + 1, dtype=jnp.int32)
    phases = samples[:, None] * frequency[None, :] % WS
    angles = phases.astype(jnp.float32) * (2.0 * math.pi / WS)
    return jnp.concatenate([jnp.cos(angles), -jnp.sin(angles)], axis=1).astype(jnp.bfloat16)


def lag_table():
    frequency = jnp.arange(1, BINS + 1, dtype=jnp.int32)
    shifts = jnp.arange(LAGS, dtype=jnp.int32) - LAGS // 2
    phases = shifts[:, None] * frequency[None, :] % WS
    angles = phases.astype(jnp.float32) * (2.0 * math.pi / WS)
    return (
        jnp.stack([jnp.cos(angles), -jnp.sin(angles)], axis=2)
        .reshape(LAGS, 2 * BINS)
        .astype(jnp.bfloat16)
    )


def whiten(windowed, polarity):
    spectra = jnp.dot(windowed, forward_table(), preferred_element_type=jnp.float32)
    power_mean = jnp.sum(spectra * spectra, axis=1) / BINS
    factor = polarity / jnp.sqrt(power_mean + 1e-06)
    return (spectra * factor[:, None]).astype(jnp.bfloat16)


def shards(record, deck_ids, partners):
    groups = lax.axis_size("blk")
    members = lax.axis_size("win")
    group_index = lax.axis_index("blk")
    member_index = lax.axis_index("win")
    block_rows = record.shape[0] // members
    slab_windows = record.shape[1] // WS
    windows = slab_windows * members
    pair_count = partners.shape[1]
    capacity = members * pair_count // groups
    all_blocks = groups * members
    listed = jnp.any(
        partners[:, :, None] == jnp.arange(all_blocks, dtype=jnp.int32)[None, None, :], axis=1
    )
    needed = jnp.any(listed.reshape(groups, members, groups, members), axis=1)
    ranked = jnp.cumsum(needed.astype(jnp.int32), axis=2) - 1
    needed_here = lax.dynamic_index_in_dim(needed, group_index, 1, keepdims=False)
    ranked_here = lax.dynamic_index_in_dim(ranked, group_index, 1, keepdims=False)
    chosen = needed_here[:, None, :] & (
        ranked_here[:, None, :] == jnp.arange(capacity, dtype=jnp.int32)[None, :, None]
    )
    slot_member = jnp.sum(
        jnp.where(chosen, jnp.arange(members, dtype=jnp.int32)[None, None, :], 0), axis=2
    )
    group_rows = lax.dynamic_slice_in_dim(partners, group_index * members, members, 0)
    source = group_rows // members
    ranked_mine = lax.dynamic_index_in_dim(ranked, group_index, 0, keepdims=False)
    slot_rank = jnp.take(
        ranked_mine.reshape(-1), (source * members + group_rows % members).reshape(-1)
    )
    flat_index = source.reshape(-1) * capacity + slot_rank
    payload = record.reshape(members, block_rows, slab_windows, WS)
    value_width = payload.shape[3]
    outgoing = jnp.take(payload, slot_member.reshape(-1), axis=0)
    outgoing = outgoing.reshape(groups, capacity, block_rows, slab_windows, value_width)
    incoming = lax.all_to_all(outgoing, "blk", split_axis=0, concat_axis=0, tiled=True)
    pieces = jnp.take(
        incoming.reshape(groups * capacity, block_rows, slab_windows, value_width),
        flat_index,
        axis=0,
    )
    pieces = pieces.reshape(members, pair_count, block_rows, slab_windows, value_width)
    bundle = jnp.concatenate([payload[:, None], pieces], axis=1)
    pair_items = lax.all_to_all(bundle, "win", split_axis=0, concat_axis=3, tiled=True)
    pair_items = pair_items.reshape(1 + pair_count, block_rows, windows, value_width)
    own_id = group_index * members + member_index
    own_row = lax.dynamic_index_in_dim(partners, own_id, 0, keepdims=False)
    item_ids = jnp.concatenate([own_id.reshape(1), own_row])
    polarity = jnp.repeat(
        1.0 - 2.0 * jnp.take(deck_ids, item_ids).astype(jnp.float32), block_rows * windows
    )
    spectra = whiten(pair_items.reshape(-1, WS), polarity).reshape(
        1 + pair_count, block_rows, windows, 2 * BINS
    )
    by_bins = jnp.transpose(
        spectra.reshape(1 + pair_count, block_rows, windows, 2, BINS), (0, 4, 2, 3, 1)
    )
    own_spectra = by_bins[0]
    rotated = jnp.stack([own_spectra[:, :, 1], -own_spectra[:, :, 0]], axis=2)
    left_side = jnp.concatenate([own_spectra, rotated], axis=3)
    lags = lag_table()
    lag_scale = 1.0 / math.sqrt(windows * BINS)

    def one_pair(partner):
        cross_spec = lax.dot_general(
            left_side, partner, (((1, 2), (1, 2)), ((0,), (0,))), preferred_element_type=jnp.float32
        )
        cross_spec = cross_spec.astype(jnp.bfloat16).reshape(BINS * 2, block_rows * block_rows)
        lagged = jnp.dot(lags, cross_spec, preferred_element_type=jnp.float32)
        return (lagged * lag_scale).astype(jnp.bfloat16)

    return lax.map(one_pair, by_bins[1:])


def solution(mesh):
    return jax.shard_map(
        shards,
        mesh=mesh,
        in_specs=(P("blk", "win"), P(), P()),
        out_specs=P(("blk", "win"), None, None),
        check_vma=False,
    )
```

profile of v0, /device:TPU:1, one launch (start us, length us, event | category | flops | bytes accessed | tf_op | source)
XLA Modules:
  0.0 396.2 jit_solution(1181942388106259657)
XLA Ops:
  5.4 9.9 %gather_fusion.1 = bf16[16,128,2,512]{3,2,1,0:T(2,128)(2,1)} fusion(bf16[4,128,2,512]{3,2,1,0:T(2,128)(2,1)S(1)} %reshape.414, s32[1024]{0:T(1024)S(1)} %pad_clamp_fusion.2), kind=kCustom, calls=%fused_computation.1 | custom fusion | bytes 8388672 | tf_op jit(solution)/shard_map/jit(_take)/gather | solution.py:73
  15.4 5.0 %copy.76 = bf16[16,128,2,512]{3,1,2,0:T(8,128)(2,1)} copy(bf16[16,128,2,512]{3,2,1,0:T(2,128)(2,1)} %gather_fusion.1) | data formatting | bytes 8388608 | tf_op jit(solution)/shard_map/jit(_take)/gather | solution.py:73
  20.5 4.7 %broadcast_select_fusion = bf16[8,2,128,2,512]{4,2,3,1,0:T(8,128)(2,1)} fusion(bf16[8,2,128,2,512]{4,2,3,1,0:T(8,128)(2,1)} %bitcast.63, pred[8,2]{1,0:T(8,128)(4,1)S(1)} %copy.74), kind=kLoop, calls=%fused_computation.15 | loop fusion | flops 2097152 | bytes 8388624 | tf_op jit(solution)/shard_map/jit(_take)/select_n | solution.py:73
  25.2 5.3 %all-to-all-start = ((bf16[8,2,128,2,512]{4,2,3,1,0:T(8,128)(2,1)}), bf16[8,2,128,2,512]{4,2,3,1,0:T(8,128)(2,1)}, u32[]{:S(2)}, u32[]{:S(2)}) async-start(bf16[8,2,128,2,512]{4,2,3,1,0:T(8,128)(2,1)} %broadcast_select_fusion), calls=%async_computation | async-start | bytes 8388608 | tf_op jit(solution)/shard_map/all_to_all | solution.py:75
  32.4 43.7 %all-to-all-done = bf16[8,2,128,2,512]{4,2,3,1,0:T(8,128)(2,1)} async-done(((bf16[8,2,128,2,512]{4,2,3,1,0:T(8,128)(2,1)}), bf16[8,2,128,2,512]{4,2,3,1,0:T(8,128)(2,1)}, u32[]{:S(2)}, u32[]{:S(2)}) %all-to-all-start) | async-done | bytes 4194336 | tf_op jit(solution)/shard_map/all_to_all | solution.py:75
  76.1 5.0 %gather_fusion.2 = bf16[16,128,2,512]{3,1,2,0:T(8,128)(2,1)} fusion(bf16[16,128,2,512]{3,1,2,0:T(8,128)(2,1)} %bitcast.11, s32[1024]{0:T(1024)S(1)} %pad_clamp_fusion.1), kind=kCustom, calls=%fused_computation.2 | custom fusion | bytes 8388672 | tf_op jit(solution)/shard_map/jit(_take)/gather | solution.py:76
  81.1 2.6 broadcast_select_fusion.1
  83.8 2.8 pad_maximum_fusion
  86.6 5.4 %all-to-all-start.1 = ((bf16[4,5,128,2,512]{4,2,3,1,0:T(8,128)(2,1)}), bf16[4,5,128,2,512]{4,2,3,1,0:T(8,128)(2,1)}, u32[]{:S(2)}, u32[]{:S(2)}) async-start(bf16[4,5,128,2,512]{4,2,3,1,0:T(8,128)(2,1)} %pad_maximum_fusion), calls=%async_computation.1 | async-start | bytes 10485760 | tf_op jit(solution)/shard_map/all_to_all | solution.py:83
  94.7 113.0 %all-to-all-done.1 = bf16[4,5,128,2,512]{4,2,3,1,0:T(8,128)(2,1)} async-done(((bf16[4,5,128,2,512]{4,2,3,1,0:T(8,128)(2,1)}), bf16[4,5,128,2,512]{4,2,3,1,0:T(8,128)(2,1)}, u32[]{:S(2)}, u32[]{:S(2)}) %all-to-all-start.1) | async-done | bytes 5242912 | tf_op jit(solution)/shard_map/all_to_all | solution.py:83
  207.6 10.2 %copy.78 = bf16[1,5,128,4,2,512]{5,4,3,2,1,0:T(2,128)(2,1)} copy(bf16[1,5,128,4,2,512]{5,2,4,1,3,0:T(8,128)(2,1)} %bitcast.16) | data formatting | bytes 10485760 | tf_op jit(solution)/shard_map/all_to_all | solution.py:83
  217.9 8.7 %reshape_reshape.6 = bf16[5120,512]{1,0:T(8,128)(2,1)} reshape(bf16[1,5,128,4,2,512]{5,4,3,2,1,0:T(2,128)(2,1)} %copy.78) | data formatting | bytes 10485760 | tf_op jit(solution)/shard_map/reshape;reshape | solution.py:91
  226.6 4.1 %multiply_reduce_fusion = (f32[5120]{0:T(1024)S(1)}, f32[5120,256]{0,1:T(8,128)S(1)}) fusion(bf16[5120,512]{1,0:T(8,128)(2,1)} %reshape_reshape.6, bf16[512,128]{1,0:T(8,128)(2,1)S(1)} %get-tuple-element.80, bf16[512,128]{1,0:T(8,128)(2,1)S(1)} %get-tuple-element.79), kind=kOutput, calls=%fused_computation.14 | convolution fusion | flops 1345317888 | bytes 10768384 | tf_op jit(solution)/shard_map/dot_general | solution.py:34
  231.1 2.6 copy.79
  234.8 3.3 slice.24
  239.6 155.9 %while.10 = (s32[]{:T(128)}, bf16[4,64,16384]{2,1,0:T(8,128)(2,1)}, bf16[4,128,8,2,128]{1,2,3,4,0:T(8,128)(2,1)}, bf16[128,8,2,256]{3,1,2,0:T(8,128)(2,1)S(1)}, bf16[64,256]{1,0:T(8,128)(2,1)S(1)}, /*index=5*/s32[]{:T(128)}) while((s32[]{:T(128)}, bf16[4,64,16384]{2,1,0:T(8,128)(2,1)}, bf16[4,128,8,2,128]{1,2,3,4,0:T(8,128)(2,1)}, ...), condition=%wide.region_6.7_spmd, body=%wide.region_5.6_spmd.sunk | while | flops 677380096 | bytes 56132168 | solution.py:111
  241.7 5.6 %fusion.43 = bf16[128,256,128]{1,2,0:T(8,128)(2,1)} fusion(bf16[128,8,2,256]{3,1,2,0:T(8,128)(2,1)S(1)} %get-tuple-element.131, bf16[1,128,8,2,128]{4,2,3,1,0:T(8,128)(2,1)S(1)} %copy.89), kind=kOutput, calls=%fused_computation.9.clone.1 | convolution fusion | flops 138412032 | bytes 9961472 | tf_op jit(solution)/shard_map/while/body/eval_jaxpr/dot_general | solution.py:104
  247.3 11.9 %copy.90 = bf16[128,256,128]{2,1,0:T(8,128)(2,1)} copy(bf16[128,256,128]{1,2,0:T(8,128)(2,1)} %fusion.43) | data formatting | bytes 16777216 | tf_op jit(solution)/shard_map/while/body/eval_jaxpr/convert_element_type | solution.py:107
  259.2 13.3 %reshape.454 = bf16[256,16384]{1,0:T(8,128)(2,1)} reshape(bf16[128,256,128]{2,1,0:T(8,128)(2,1)} %copy.90) | data formatting | bytes 16777216 | tf_op jit(solution)/shard_map/while/body/eval_jaxpr/reshape | solution.py:107
  272.5 6.3 %fusion.44 = bf16[4,64,16384]{2,1,0:T(8,128)(2,1)} fusion(bf16[4,64,16384]{2,1,0:T(8,128)(2,1)} %get-tuple-element.123, s32[]{:T(128)} %get-tuple-element.122, bf16[64,256]{1,0:T(8,128)(2,1)S(1)} %get-tuple-element.132, bf16[256,16384]{1,0:T(8,128)(2,1)} %reshape.454), kind=kOutput, calls=%fused_computation.7.clone.1 | convolution fusion | flops 538968064 | bytes 10519040 | tf_op jit(solution)/shard_map/while/body/eval_jaxpr/dot_general | solution.py:108
  280.6 5.6 %fusion.43 = bf16[128,256,128]{1,2,0:T(8,128)(2,1)} fusion(bf16[128,8,2,256]{3,1,2,0:T(8,128)(2,1)S(1)} %get-tuple-element.131, bf16[1,128,8,2,128]{4,2,3,1,0:T(8,128)(2,1)S(1)} %copy.89), kind=kOutput, calls=%fused_computation.9.clone.1 | convolution fusion | flops 138412032 | bytes 9961472 | tf_op jit(solution)/shard_map/while/body/eval_jaxpr/dot_general | solution.py:104
  286.2 11.9 %copy.90 = bf16[128,256,128]{2,1,0:T(8,128)(2,1)} copy(bf16[128,256,128]{1,2,0:T(8,128)(2,1)} %fusion.43) | data formatting | bytes 16777216 | tf_op jit(solution)/shard_map/while/body/eval_jaxpr/convert_element_type | solution.py:107
  298.1 13.3 %reshape.454 = bf16[256,16384]{1,0:T(8,128)(2,1)} reshape(bf16[128,256,128]{2,1,0:T(8,128)(2,1)} %copy.90) | data formatting | bytes 16777216 | tf_op jit(solution)/shard_map/while/body/eval_jaxpr/reshape | solution.py:107
  311.4 6.3 %fusion.44 = bf16[4,64,16384]{2,1,0:T(8,128)(2,1)} fusion(bf16[4,64,16384]{2,1,0:T(8,128)(2,1)} %get-tuple-element.123, s32[]{:T(128)} %get-tuple-element.122, bf16[64,256]{1,0:T(8,128)(2,1)S(1)} %get-tuple-element.132, bf16[256,16384]{1,0:T(8,128)(2,1)} %reshape.454), kind=kOutput, calls=%fused_computation.7.clone.1 | convolution fusion | flops 538968064 | bytes 10519040 | tf_op jit(solution)/shard_map/while/body/eval_jaxpr/dot_general | solution.py:108
  319.5 5.6 %fusion.43 = bf16[128,256,128]{1,2,0:T(8,128)(2,1)} fusion(bf16[128,8,2,256]{3,1,2,0:T(8,128)(2,1)S(1)} %get-tuple-element.131, bf16[1,128,8,2,128]{4,2,3,1,0:T(8,128)(2,1)S(1)} %copy.89), kind=kOutput, calls=%fused_computation.9.clone.1 | convolution fusion | flops 138412032 | bytes 9961472 | tf_op jit(solution)/shard_map/while/body/eval_jaxpr/dot_general | solution.py:104
  325.1 11.9 %copy.90 = bf16[128,256,128]{2,1,0:T(8,128)(2,1)} copy(bf16[128,256,128]{1,2,0:T(8,128)(2,1)} %fusion.43) | data formatting | bytes 16777216 | tf_op jit(solution)/shard_map/while/body/eval_jaxpr/convert_element_type | solution.py:107
  337.0 13.3 %reshape.454 = bf16[256,16384]{1,0:T(8,128)(2,1)} reshape(bf16[128,256,128]{2,1,0:T(8,128)(2,1)} %copy.90) | data formatting | bytes 16777216 | tf_op jit(solution)/shard_map/while/body/eval_jaxpr/reshape | solution.py:107
  350.3 6.3 %fusion.44 = bf16[4,64,16384]{2,1,0:T(8,128)(2,1)} fusion(bf16[4,64,16384]{2,1,0:T(8,128)(2,1)} %get-tuple-element.123, s32[]{:T(128)} %get-tuple-element.122, bf16[64,256]{1,0:T(8,128)(2,1)S(1)} %get-tuple-element.132, bf16[256,16384]{1,0:T(8,128)(2,1)} %reshape.454), kind=kOutput, calls=%fused_computation.7.clone.1 | convolution fusion | flops 538968064 | bytes 10519040 | tf_op jit(solution)/shard_map/while/body/eval_jaxpr/dot_general | solution.py:108
  358.4 5.6 %fusion.43 = bf16[128,256,128]{1,2,0:T(8,128)(2,1)} fusion(bf16[128,8,2,256]{3,1,2,0:T(8,128)(2,1)S(1)} %get-tuple-element.131, bf16[1,128,8,2,128]{4,2,3,1,0:T(8,128)(2,1)S(1)} %copy.89), kind=kOutput, calls=%fused_computation.9.clone.1 | convolution fusion | flops 138412032 | bytes 9961472 | tf_op jit(solution)/shard_map/while/body/eval_jaxpr/dot_general | solution.py:104
  364.0 11.9 %copy.90 = bf16[128,256,128]{2,1,0:T(8,128)(2,1)} copy(bf16[128,256,128]{1,2,0:T(8,128)(2,1)} %fusion.43) | data formatting | bytes 16777216 | tf_op jit(solution)/shard_map/while/body/eval_jaxpr/convert_element_type | solution.py:107
  375.9 13.3 %reshape.454 = bf16[256,16384]{1,0:T(8,128)(2,1)} reshape(bf16[128,256,128]{2,1,0:T(8,128)(2,1)} %copy.90) | data formatting | bytes 16777216 | tf_op jit(solution)/shard_map/while/body/eval_jaxpr/reshape | solution.py:107
  389.2 6.3 %fusion.44 = bf16[4,64,16384]{2,1,0:T(8,128)(2,1)} fusion(bf16[4,64,16384]{2,1,0:T(8,128)(2,1)} %get-tuple-element.123, s32[]{:T(128)} %get-tuple-element.122, bf16[64,256]{1,0:T(8,128)(2,1)S(1)} %get-tuple-element.132, bf16[256,16384]{1,0:T(8,128)(2,1)} %reshape.454), kind=kOutput, calls=%fused_computation.7.clone.1 | convolution fusion | flops 538968064 | bytes 10519040 | tf_op jit(solution)/shard_map/while/body/eval_jaxpr/dot_general | solution.py:108
  (70 shorter events, 21.0 us)
Async XLA Ops:
  0.0 92.3 %copy-start = (s32[32]{0:T(128)S(1)}, s32[32]{0:T(128)}, u32[]{:S(2)}) copy-start(s32[32]{0:T(128)} %param.6) | copy-start | bytes 388
  25.2 5.3 %copy-start.2 = (bf16[512,1024]{1,0:T(8,128)(2,1)S(1)}, bf16[512,1024]{1,0:T(8,128)(2,1)}, u32[]{:S(2)}) copy-start(bf16[512,1024]{1,0:T(8,128)(2,1)} %param.5) | copy-start | bytes 3145732
  25.2 50.9 %all-to-all-start = ((bf16[8,2,128,2,512]{4,2,3,1,0:T(8,128)(2,1)}), bf16[8,2,128,2,512]{4,2,3,1,0:T(8,128)(2,1)}, u32[]{:S(2)}, u32[]{:S(2)}) async-start(bf16[8,2,128,2,512]{4,2,3,1,0:T(8,128)(2,1)} %broadcast_select_fusion), calls=%async_computation | async-start | bytes 8388608 | tf_op jit(solution)/shard_map/all_to_all | solution.py:75
  86.6 5.4 %copy-start.3 = (s32[32,4]{0,1:T(4,128)S(1)}, s32[32,4]{0,1:T(4,128)}, u32[]{:S(2)}) copy-start(s32[32,4]{0,1:T(4,128)} %param.7) | copy-start | bytes 1540
  86.6 121.1 %all-to-all-start.1 = ((bf16[4,5,128,2,512]{4,2,3,1,0:T(8,128)(2,1)}), bf16[4,5,128,2,512]{4,2,3,1,0:T(8,128)(2,1)}, u32[]{:S(2)}, u32[]{:S(2)}) async-start(bf16[4,5,128,2,512]{4,2,3,1,0:T(8,128)(2,1)} %pad_maximum_fusion), calls=%async_computation.1 | async-start | bytes 10485760 | tf_op jit(solution)/shard_map/all_to_all | solution.py:83
  395.5 0.7 copy-start.1
where the time goes:
time: 402 us; the launch traced here: 396 us
  local copies, waits for them, and re-layouts  162 us (40%)
  waiting for transfers between devices  157 us (39%)
  matrix products  51.6 us (13%)
  other arithmetic  14.5 us (4%)
  starting transfers between devices  10.6 us (3%)
    all_to_all x1, waiting for transfers between devices, shards(): lax.all_to_all(bundle, 'win', split_axis=0, concat_axis=3, tiled=True)  113 us
    reshape x4, local copies, waits for them, and re-layouts, one_pair(): cross_spec.astype(jnp.bfloat16).reshape(BINS * 2, block_rows * block_rows)  53.2 us
    convert_element_type x4, local copies, waits for them, and re-layouts, one_pair(): cross_spec.astype(jnp.bfloat16).reshape(BINS * 2, block_rows * block_rows)  47.7 us
    all_to_all x1, waiting for transfers between devices, shards(): lax.all_to_all(outgoing, 'blk', split_axis=0, concat_axis=0, tiled=True)  43.7 us
    dot_general x4, matrix products, one_pair(): lagged = jnp.dot(lags, cross_spec, preferred_element_type=jnp.float32)  25.1 us
    dot_general x4, matrix products, one_pair(): lax.dot_general(left_side, partner, (((1, 2), (1, 2)), ((0,), (0,))), pre...  22.3 us
    gather x2, local copies, waits for them, and re-layouts, shards(): outgoing = jnp.take(payload, slot_member.reshape(-1), axis=0)  15 us
    all_to_all x1, local copies, waits for them, and re-layouts, shards(): lax.all_to_all(bundle, 'win', split_axis=0, concat_axis=3, tiled=True)  10.2 us
  transfers between devices with their start and end apart: 2, of which 2 were waited for; matrix products, arithmetic and copies ran while one was open for 1% of the time, Pallas kernels for 0%

commit v1 on v0

v1 whole, which is shorter than its diff:
```python
import functools
import math

import jax
import jax.numpy as jnp
import numpy as np
from jax import lax
from jax.experimental import pallas as pl
from jax.experimental.pallas import tpu as pltpu
from jax.sharding import PartitionSpec as P

WS = 512
BINS = 128
LAGS = 64
PIECE_ROWS = 16
TILE = 8


def forward_table():
    phases = np.arange(WS)[:, None] * np.arange(1, BINS + 1)[None, :] % WS
    angles = phases * (2.0 * math.pi / WS)
    return jnp.asarray(np.concatenate([np.cos(angles), -np.sin(angles)], axis=1), jnp.bfloat16)


def lag_table(scale):
    shifts = np.arange(LAGS) - LAGS // 2
    phases = shifts[:, None] * np.arange(1, BINS + 1)[None, :] % WS
    angles = phases * (2.0 * math.pi / WS)
    table = np.stack([np.cos(angles), -np.sin(angles)], axis=0)
    return jnp.asarray(table, jnp.bfloat16).astype(jnp.float32) * scale


def whiten_kernel(block_rows, deck_ref, record_ref, table_ref, out_ref):
    pieces, blocks, rows, lanes = out_ref.shape
    windows = record_ref.shape[1] // WS
    lane_parts = windows * 2 * BINS // lanes
    for block in range(blocks):
        here = pl.ds(block * block_rows, block_rows)
        polarity = (1 - 2 * deck_ref[block]).astype(jnp.float32)
        values = []
        for window in range(windows):
            spectra = jnp.dot(
                record_ref[here, pl.ds(window * WS, WS)],
                table_ref[...],
                preferred_element_type=jnp.float32,
            )
            power = jnp.sum(spectra * spectra, axis=1, keepdims=True) / BINS
            values.append((spectra * (polarity / jnp.sqrt(power + 1e-06))).astype(jnp.bfloat16))
        whole = jnp.concatenate(values, axis=1)
        for piece in range(pieces):
            row, lane = piece // lane_parts, piece % lane_parts
            out_ref[piece, block] = whole[
                row * rows : (row + 1) * rows, lane * lanes : (lane + 1) * lanes
            ]


def whiten(record, decks, pieces, block_rows, rows, lanes):
    blocks = record.shape[0] // block_rows
    return pl.pallas_call(
        functools.partial(whiten_kernel, block_rows),
        out_shape=jax.ShapeDtypeStruct((pieces, blocks, rows, lanes), jnp.bfloat16),
        in_specs=[
            pl.BlockSpec(memory_space=pltpu.SMEM),
            pl.BlockSpec(memory_space=pltpu.VMEM),
            pl.BlockSpec(memory_space=pltpu.VMEM),
        ],
        out_specs=pl.BlockSpec(memory_space=pltpu.VMEM),
        compiler_params=pltpu.CompilerParams(vmem_limit_bytes=32 * 2**20),
    )(decks, record, forward_table())


def pick_kernel(ids_ref, full_ref, out_ref, sems):
    copies = []
    for item in range(out_ref.shape[0]):
        copies.append(
            pltpu.make_async_copy(full_ref.at[:, ids_ref[item]], out_ref.at[item], sems.at[item])
        )
        copies[-1].start()
    for copy in copies:
        copy.wait()


def pick(ids, full):
    slabs, _, rows, lanes = full.shape
    return pl.pallas_call(
        pick_kernel,
        out_shape=jax.ShapeDtypeStruct((ids.shape[0], slabs, rows, lanes), full.dtype),
        in_specs=[
            pl.BlockSpec(memory_space=pltpu.SMEM),
            pl.BlockSpec(memory_space=pl.ANY),
        ],
        out_specs=pl.BlockSpec(memory_space=pl.ANY),
        scratch_shapes=[pltpu.SemaphoreType.DMA((ids.shape[0],))],
    )(ids, full)


def correlate_kernel(lane_parts, items_ref, lags_ref, out_ref, own, partners, even, odd):
    pieces, blocks, slabs, rows, lanes = items_ref.shape
    step = pl.program_id(0)
    pairs = blocks - 1
    depth = own.shape[1]
    block_rows = own.shape[0]
    slab_lanes = lanes * lane_parts

    def shift(buffer, first):
        cosine, sine = lags_ref[0], lags_ref[1]
        for row in range(TILE):
            line = own[pl.ds(first + row, 1), :]
            for window in range(depth // (2 * BINS)):
                base = window * 2 * BINS
                real = line[:, base : base + BINS]
                imag = line[:, base + BINS : base + 2 * BINS]
                buffer[row * LAGS : (row + 1) * LAGS, base : base + BINS] = (
                    real * cosine + imag * sine
                ).astype(jnp.bfloat16)
                buffer[row * LAGS : (row + 1) * LAGS, base + BINS : base + 2 * BINS] = (
                    imag * cosine - real * sine
                ).astype(jnp.bfloat16)

    def multiply(buffer, first):
        total = jnp.dot(buffer[...], partners[...], preferred_element_type=jnp.float32)
        total = total.astype(jnp.bfloat16)
        for row in range(TILE):
            for pair in range(pairs):
                out_ref[pair, :, (first + row) * block_rows : (first + row + 1) * block_rows] = (
                    total[row * LAGS : (row + 1) * LAGS, pair * block_rows : (pair + 1) * block_rows]
                )

    @pl.when(step == 0)
    def _():
        for slab in range(slabs):
            for lane in range(lane_parts):
                at = slab * slab_lanes + lane * lanes
                parts = range(lane, pieces, lane_parts)
                mine = jnp.concatenate([items_ref[part, 0, slab] for part in parts], axis=0)
                own[:, at : at + lanes] = mine.astype(jnp.float32)
                for pair in range(pairs):
                    other = jnp.concatenate(
                        [items_ref[part, 1 + pair, slab] for part in parts], axis=0
                    )
                    partners[at : at + lanes, pair * block_rows : (pair + 1) * block_rows] = other.T
        shift(even, 0)

    first = step * 2 * TILE
    shift(odd, first + TILE)
    multiply(even, 0)
    shift(even, lax.rem(first + 2 * TILE, block_rows))
    multiply(odd, TILE)


def correlate(items, block_rows, lane_parts):
    pieces, blocks, slabs, rows, lanes = items.shape
    pairs = blocks - 1
    depth = slabs * lanes * lane_parts
    windows = depth // (2 * BINS)
    scale = 1.0 / math.sqrt(windows * BINS)
    return pl.pallas_call(
        functools.partial(correlate_kernel, lane_parts),
        grid=(block_rows // (2 * TILE),),
        out_shape=jax.ShapeDtypeStruct((pairs, LAGS, block_rows * block_rows), jnp.bfloat16),
        in_specs=[
            pl.BlockSpec(memory_space=pltpu.VMEM),
            pl.BlockSpec(memory_space=pltpu.VMEM),
        ],
        out_specs=pl.BlockSpec((pairs, LAGS, 2 * TILE * block_rows), lambda i: (0, 0, i)),
        scratch_shapes=[
            pltpu.VMEM((block_rows, depth), jnp.float32),
            pltpu.VMEM((depth, pairs * block_rows), jnp.bfloat16),
            pltpu.VMEM((TILE * LAGS, depth), jnp.bfloat16),
            pltpu.VMEM((TILE * LAGS, depth), jnp.bfloat16),
        ],
        compiler_params=pltpu.CompilerParams(vmem_limit_bytes=48 * 2**20),
        cost_estimate=pl.CostEstimate(
            flops=2 * LAGS * block_rows * depth * pairs * block_rows,
            bytes_accessed=pairs * LAGS * block_rows * block_rows * 2,
            transcendentals=0,
        ),
    )(items, lag_table(scale))


def shards(record, deck_ids, partners):
    groups = lax.axis_size("blk")
    members = lax.axis_size("win")
    group_index = lax.axis_index("blk")
    member_index = lax.axis_index("win")
    block_rows = record.shape[0] // members
    slab_lanes = record.shape[1] // WS * 2 * BINS
    row_parts = block_rows // PIECE_ROWS
    lane_parts = max(1, groups // row_parts)
    lanes = slab_lanes // lane_parts
    rows = block_rows * lane_parts // groups
    all_blocks = groups * members
    decks = lax.dynamic_slice_in_dim(deck_ids, group_index * members, members, 0)
    pieces = whiten(record, decks, groups, block_rows, rows, lanes)
    held = lax.all_to_all(pieces, "blk", split_axis=0, concat_axis=0, tiled=True)
    held = held.reshape(all_blocks, rows, lanes)
    full = lax.all_gather(held, "win", axis=0)
    own_ids = jnp.arange(groups, dtype=jnp.int32) * members + member_index
    rows_here = lax.dynamic_index_in_dim(
        partners.reshape(groups, members, -1), member_index, 1, keepdims=False
    )
    ids = jnp.concatenate([own_ids[:, None], rows_here], axis=1)
    chosen = pick(ids.reshape(-1), full)
    chosen = chosen.reshape(groups, ids.shape[1], members, rows, lanes)
    items = lax.all_to_all(chosen, "blk", split_axis=0, concat_axis=0, tiled=True)
    return correlate(items, block_rows, lane_parts)


def solution(mesh):
    return jax.shard_map(
        shards,
        mesh=mesh,
        in_specs=(P("blk", "win"), P(), P()),
        out_specs=P(("blk", "win"), None, None),
        check_vma=False,
    )
```

time: 402 us -> 217 us (0.54); the launches traced: 396 us -> 216 us
  local copies, waits for them, and re-layouts: 162 us -> 3.98 us
  waiting for transfers between devices: 157 us -> 45 us
  Pallas kernels: 0 us -> 104 us
  matrix products: 51.6 us -> 0 us
  blocking collectives: 0 us -> 48.9 us
  other arithmetic: 14.5 us -> 0.02 us
  between operations: 0.23 us -> 13.4 us
  starting transfers between devices: 10.6 us -> 0.01 us
    all_to_all x2 -> x0, waiting for transfers between devices: 157 us -> none  [the longest x1 113 us: shards(): lax.all_to_all(bundle, 'win', split_axis=0, concat_axis=3, tiled=True)]
    pallas_call x0 -> x3, Pallas kernels: none -> 104 us  [the longest x1 81.5 us: pick(): pl.pallas_call(pick_kernel, out_shape=jax.ShapeDtypeStruct((ids.shape[0],...]
    reshape x10 -> x2, local copies, waits for them, and re-layouts: 55.4 us -> 0.75 us  [the longest x1 0.67 us: shards(): chosen = pick(ids.reshape(-1), full)]
    dot_general x9 -> x0, matrix products: 51.6 us -> none  [the longest x4 25.1 us: one_pair(): lagged = jnp.dot(lags, cross_spec, preferred_element_type=jnp.float32)]
    convert_element_type x5 -> x0, local copies, waits for them, and re-layouts: 50.3 us -> none  [the longest x4 47.7 us: one_pair(): cross_spec.astype(jnp.bfloat16).reshape(BINS * 2, block_rows * block_rows)]
    all_to_all x0 -> x2, blocking collectives: none -> 48.9 us  [the longest x1 35.4 us: shards(): lax.all_to_all(chosen, 'blk', split_axis=0, concat_axis=0, tiled=True)]
    all_gather x0 -> x1, waiting for transfers between devices: none -> 45 us  [shards(): full = lax.all_gather(held, 'win', axis=0)]
    gather x6 -> x0, local copies, waits for them, and re-layouts: 21.4 us -> none  [the longest x2 15 us: shards(): outgoing = jnp.take(payload, slot_member.reshape(-1), axis=0)]
  transfers between devices with their start and end apart: 2 -> 1, of which waited for: 2 -> 1; matrix products, arithmetic and copies ran while one was open for 1% -> 0% of each run, Pallas kernels for 0% -> 0%
where the time goes in v1:
time: 217 us; the launch traced here: 216 us
  Pallas kernels  104 us (48%)
  blocking collectives  48.9 us (23%)
  waiting for transfers between devices  45 us (21%)
  between operations  13.4 us (6%)
  local copies, waits for them, and re-layouts  3.98 us (2%)
    pallas_call x1, Pallas kernels, pick(): pl.pallas_call(pick_kernel, out_shape=jax.ShapeDtypeStruct((ids.shape[0],...  81.5 us
    all_gather x1, waiting for transfers between devices, shards(): full = lax.all_gather(held, 'win', axis=0)  45 us
    all_to_all x1, blocking collectives, shards(): lax.all_to_all(chosen, 'blk', split_axis=0, concat_axis=0, tiled=True)  35.4 us
    pallas_call x1, Pallas kernels, correlate(): pl.pallas_call(functools.partial(correlate_kernel, lane_parts), grid=(blo...  21.6 us
    all_to_all x1, blocking collectives, shards(): lax.all_to_all(pieces, 'blk', split_axis=0, concat_axis=0, tiled=True)  13.5 us
  transfers between devices with their start and end apart: 1, of which 1 were waited for; matrix products, arithmetic and copies ran while one was open for 0% of the time, Pallas kernels for 0%

profile of v1, /device:TPU:1, one launch (start us, length us, event | category | flops | bytes accessed | tf_op | source)
XLA Modules:
  0.0 215.6 jit_solution(17129300738722918669)
XLA Ops:
  6.5 0.0 copy-start.3
  6.5 0.0 all-gather.2.cloned.1.call-start
  6.5 0.7 dynamic_slice.8.deck_ref
  7.3 0.0 copy-start
  7.3 1.2 copy-done
  8.5 0.0 copy-start.1
  8.5 0.9 copy-done.1
  9.5 1.1 shard_map.55
  10.6 13.5 %all_to_all.10 = bf16[8,4,16,512]{3,2,1,0:T(8,128)(2,1)} all-to-all(bf16[8,4,16,512]{3,2,1,0:T(8,128)(2,1)S(1)} %shard_map.55), channel_id=1, replica_groups=mesh['blk'=8,'win'=4] {'blk'}, dimensions={0} | all-to-all | bytes 1048576 | tf_op jit(solution)/shard_map/all_to_all | solution.py:195
  24.1 0.0 all-gather.2.cloned.1.call-update
  24.1 0.0 copy-done.3
  24.2 0.1 reshape.19
  24.2 0.2 dynamic-slice_reduce_fusion
  24.5 0.1 copy.8
  24.6 0.7 reshape.20.ids_ref
  25.2 45.0 %all-gather.2.cloned.1.call-done.full_ref = bf16[4,32,16,512]{3,2,1,0:T(8,128)(2,1)} async-done(((bf16[1,32,16,512]{3,2,1,0:T(8,128)(2,1)}), bf16[4,32,16,512]{3,2,1,0:T(8,128)(2,1)}) %all-gather.2.cloned.1.call-update) | async-done | bytes 2097168 | tf_op jit(solution)/shard_map/all_gather | solution.py:197
  70.2 81.5 %shard_map.56 = bf16[40,4,16,512]{3,2,1,0:T(8,128)(2,1)} custom-call(s32[40]{0:T(128)} %reshape.20.ids_ref, bf16[4,32,16,512]{3,2,1,0:T(8,128)(2,1)} %all-gather.2.cloned.1.call-done.full_ref), custom_call_target="tpu_custom_call" | custom-call | tf_op jit(solution)/shard_map/pallas_call | solution.py:85
  151.8 0.0 copy-start.2
  151.8 35.4 %all_to_all.11.items_ref = bf16[8,5,4,16,512]{4,3,2,1,0:T(8,128)(2,1)S(1)} all-to-all(bf16[8,5,4,16,512]{4,3,2,1,0:T(8,128)(2,1)} %bitcast.4), channel_id=1, replica_groups=mesh['blk'=8,'win'=4] {'blk'}, dimensions={0} | all-to-all | bytes 5242880 | tf_op jit(solution)/shard_map/all_to_all | solution.py:205
  187.2 0.0 copy-done.2
  187.2 21.6 %shard_map.57 = bf16[4,64,16384]{2,1,0:T(8,128)(2,1)} custom-call(bf16[8,5,4,16,512]{4,3,2,1,0:T(8,128)(2,1)S(1)} %all_to_all.11.items_ref, f32[2,64,128]{2,1,0:T(8,128)S(1)} %copy-done.2), custom_call_target="tpu_custom_call" | custom-call | flops 17179869184 | bytes 8388608 | tf_op jit(solution)/shard_map/pallas_call | solution.py:157
  (2 shorter events, 0.0 us)
Async XLA Ops:
  6.5 17.6 %copy-start.3 = (s32[32,4]{0,1:T(4,128)S(1)}, s32[32,4]{0,1:T(4,128)}, u32[]{:S(2)}) copy-start(s32[32,4]{0,1:T(4,128)} %param.7) | copy-start | bytes 1540
  6.5 63.7 %all-gather.2.cloned.1.call-start = ((), (), s32[]{:S(2)}) async-start(), calls=%async_computation.2 | async-start | bytes 2621440 | tf_op jit(solution)/shard_map/all_gather | solution.py:197
  7.3 1.2 copy-start
  8.5 0.9 copy-start.1
  151.8 35.4 %copy-start.2 = (f32[2,64,128]{2,1,0:T(8,128)S(1)}, f32[2,64,128]{2,1,0:T(8,128)}, u32[]{:S(2)}) copy-start(f32[2,64,128]{2,1,0:T(8,128)} %constant.29.lags_ref) | copy-start | bytes 196612
Sparse Core Ops, SparseCore 0:
  24.3 45.9 all-gather.1

commit v2 on v1

--- a/solution.py
+++ b/solution.py
@@ -69,15 +69,12 @@
     )(decks, record, forward_table())
 
 
-def pick_kernel(ids_ref, full_ref, out_ref, sems):
-    copies = []
-    for item in range(out_ref.shape[0]):
-        copies.append(
-            pltpu.make_async_copy(full_ref.at[:, ids_ref[item]], out_ref.at[item], sems.at[item])
-        )
-        copies[-1].start()
-    for copy in copies:
-        copy.wait()
+def pick_kernel(ids_ref, full_ref, out_ref):
+    def one_item(item, carry):
+        out_ref[item] = full_ref[:, ids_ref[item]]
+        return carry
+
+    lax.fori_loop(0, out_ref.shape[0], one_item, 0)
 
 
 def pick(ids, full):
@@ -87,10 +84,10 @@
         out_shape=jax.ShapeDtypeStruct((ids.shape[0], slabs, rows, lanes), full.dtype),
         in_specs=[
             pl.BlockSpec(memory_space=pltpu.SMEM),
-            pl.BlockSpec(memory_space=pl.ANY),
-        ],
-        out_specs=pl.BlockSpec(memory_space=pl.ANY),
-        scratch_shapes=[pltpu.SemaphoreType.DMA((ids.shape[0],))],
+            pl.BlockSpec(memory_space=pltpu.VMEM),
+        ],
+        out_specs=pl.BlockSpec(memory_space=pltpu.VMEM),
+        compiler_params=pltpu.CompilerParams(vmem_limit_bytes=32 * 2**20),
     )(ids, full)
 
 

time: 217 us -> 138 us (0.64)
  Pallas kernels: 104 us -> 23.6 us
    pallas_call x1, Pallas kernels: 81.5 us -> 0.9 us  [pick(): pl.pallas_call(pick_kernel, out_shape=jax.ShapeDtypeStruct((ids.shape[0],...]
where the time goes in v2:
time: 138 us; the launch traced here: 136 us
  blocking collectives  48.7 us (35%)
  waiting for transfers between devices  45.6 us (33%)
  Pallas kernels  23.6 us (17%)
  between operations  13.4 us (10%)
  local copies, waits for them, and re-layouts  4.97 us (4%)
    all_gather x1, waiting for transfers between devices, shards(): full = lax.all_gather(held, 'win', axis=0)  45.6 us
    all_to_all x1, blocking collectives, shards(): lax.all_to_all(chosen, 'blk', split_axis=0, concat_axis=0, tiled=True)  35.2 us
    pallas_call x1, Pallas kernels, correlate(): pl.pallas_call(functools.partial(correlate_kernel, lane_parts), grid=(blo...  21.6 us
    all_to_all x1, blocking collectives, shards(): lax.all_to_all(pieces, 'blk', split_axis=0, concat_axis=0, tiled=True)  13.5 us
    unnamed x10, local copies, waits for them, and re-layouts  3.77 us
  transfers between devices with their start and end apart: 1, of which 1 were waited for; matrix products, arithmetic and copies ran while one was open for 0% of the time, Pallas kernels for 0%

profile of v2, /device:TPU:1, one launch (start us, length us, event | category | flops | bytes accessed | tf_op | source)
XLA Modules:
  0.0 136.4 jit_solution(8438096438400851228)
XLA Ops:
  6.5 0.0 copy-start.4
  6.5 0.0 all-gather.2.cloned.1.call-start
  6.5 0.7 dynamic_slice.8.deck_ref
  7.3 0.0 copy-start.1
  7.3 1.2 copy-done.1
  8.5 0.0 copy-start.2
  8.5 0.9 copy-done.2
  9.5 1.1 shard_map.55
  10.6 13.5 %all_to_all.10 = bf16[8,4,16,512]{3,2,1,0:T(8,128)(2,1)} all-to-all(bf16[8,4,16,512]{3,2,1,0:T(8,128)(2,1)S(1)} %shard_map.55), channel_id=1, replica_groups=mesh['blk'=8,'win'=4] {'blk'}, dimensions={0} | all-to-all | bytes 1048576 | tf_op jit(solution)/shard_map/all_to_all | solution.py:192
  24.1 0.0 all-gather.2.cloned.1.call-update
  24.1 0.0 copy-done.4
  24.2 0.1 reshape.19
  24.2 0.2 dynamic-slice_reduce_fusion
  24.5 0.1 copy.8
  24.6 0.1 reshape.20.ids_ref
  24.7 45.6 %all-gather.2.cloned.1.call-done.full_ref = bf16[4,32,16,512]{3,2,1,0:T(8,128)(2,1)} async-done(((bf16[1,32,16,512]{3,2,1,0:T(8,128)(2,1)}), bf16[4,32,16,512]{3,2,1,0:T(8,128)(2,1)}) %all-gather.2.cloned.1.call-update) | async-done | bytes 2097168 | tf_op jit(solution)/shard_map/all_gather | solution.py:194
  70.2 0.0 copy-start
  70.2 1.6 %copy-done = bf16[4,32,16,512]{3,2,1,0:T(8,128)(2,1)S(1)} copy-done((bf16[4,32,16,512]{3,2,1,0:T(8,128)(2,1)S(1)}, bf16[4,32,16,512]{3,2,1,0:T(8,128)(2,1)}, u32[]{:S(2)}) %copy-start) | copy-done | bytes 2097176
  71.8 0.9 shard_map.56
  72.7 0.0 copy-start.3
  72.8 35.2 %all_to_all.11.items_ref = bf16[8,5,4,16,512]{4,3,2,1,0:T(8,128)(2,1)S(1)} all-to-all(bf16[8,5,4,16,512]{4,3,2,1,0:T(8,128)(2,1)S(1)} %bitcast.4), channel_id=1, replica_groups=mesh['blk'=8,'win'=4] {'blk'}, dimensions={0} | all-to-all | bytes 5242880 | tf_op jit(solution)/shard_map/all_to_all | solution.py:202
  107.9 0.0 copy-done.3
  107.9 21.6 %shard_map.57 = bf16[4,64,16384]{2,1,0:T(8,128)(2,1)} custom-call(bf16[8,5,4,16,512]{4,3,2,1,0:T(8,128)(2,1)S(1)} %all_to_all.11.items_ref, f32[2,64,128]{2,1,0:T(8,128)S(1)} %copy-done.3), custom_call_target="tpu_custom_call" | custom-call | flops 17179869184 | bytes 8388608 | tf_op jit(solution)/shard_map/pallas_call | solution.py:154
  (2 shorter events, 0.0 us)
Async XLA Ops:
  6.5 17.6 %copy-start.4 = (s32[32,4]{0,1:T(4,128)S(1)}, s32[32,4]{0,1:T(4,128)}, u32[]{:S(2)}) copy-start(s32[32,4]{0,1:T(4,128)} %param.7) | copy-start | bytes 1540
  6.5 63.7 %all-gather.2.cloned.1.call-start = ((), (), s32[]{:S(2)}) async-start(), calls=%async_computation.2 | async-start | bytes 2621440 | tf_op jit(solution)/shard_map/all_gather | solution.py:194
  7.3 1.2 copy-start.1
  8.5 0.9 copy-start.2
  70.2 1.6 %copy-start = (bf16[4,32,16,512]{3,2,1,0:T(8,128)(2,1)S(1)}, bf16[4,32,16,512]{3,2,1,0:T(8,128)(2,1)}, u32[]{:S(2)}) copy-start(bf16[4,32,16,512]{3,2,1,0:T(8,128)(2,1)} %all-gather.2.cloned.1.call-done.full_ref) | copy-start | bytes 6291460
  72.7 35.2 %copy-start.3 = (f32[2,64,128]{2,1,0:T(8,128)S(1)}, f32[2,64,128]{2,1,0:T(8,128)}, u32[]{:S(2)}) copy-start(f32[2,64,128]{2,1,0:T(8,128)} %constant.29.lags_ref) | copy-start | bytes 196612
Sparse Core Ops, SparseCore 0:
  24.3 45.9 all-gather.1

commit v3 on v1

--- a/solution.py
+++ b/solution.py
@@ -13,6 +13,7 @@
 BINS = 128
 LAGS = 64
 PIECE_ROWS = 16
+LANES = 128
 TILE = 8
 
 
@@ -31,9 +32,9 @@
 
 
 def whiten_kernel(block_rows, deck_ref, record_ref, table_ref, out_ref):
-    pieces, blocks, rows, lanes = out_ref.shape
+    chunks, pieces, blocks, rows, chunk_lanes = out_ref.shape
     windows = record_ref.shape[1] // WS
-    lane_parts = windows * 2 * BINS // lanes
+    lane_parts = windows * 2 * BINS // (chunks * chunk_lanes)
     for block in range(blocks):
         here = pl.ds(block * block_rows, block_rows)
         polarity = (1 - 2 * deck_ref[block]).astype(jnp.float32)
@@ -49,16 +50,17 @@
         whole = jnp.concatenate(values, axis=1)
         for piece in range(pieces):
             row, lane = piece // lane_parts, piece % lane_parts
-            out_ref[piece, block] = whole[
-                row * rows : (row + 1) * rows, lane * lanes : (lane + 1) * lanes
-            ]
-
-
-def whiten(record, decks, pieces, block_rows, rows, lanes):
-    blocks = record.shape[0] // block_rows
+            for chunk in range(chunks):
+                at = (lane * chunks + chunk) * chunk_lanes
+                out_ref[chunk, piece, block] = whole[
+                    row * rows : (row + 1) * rows, at : at + chunk_lanes
+                ]
+
+
+def whiten(record, decks, block_rows, shape):
     return pl.pallas_call(
         functools.partial(whiten_kernel, block_rows),
-        out_shape=jax.ShapeDtypeStruct((pieces, blocks, rows, lanes), jnp.bfloat16),
+        out_shape=jax.ShapeDtypeStruct(shape, jnp.bfloat16),
         in_specs=[
             pl.BlockSpec(memory_space=pltpu.SMEM),
             pl.BlockSpec(memory_space=pltpu.VMEM),
@@ -69,38 +71,212 @@
     )(decks, record, forward_table())
 
 
-def pick_kernel(ids_ref, full_ref, out_ref, sems):
-    copies = []
-    for item in range(out_ref.shape[0]):
-        copies.append(
-            pltpu.make_async_copy(full_ref.at[:, ids_ref[item]], out_ref.at[item], sems.at[item])
-        )
-        copies[-1].start()
-    for copy in copies:
-        copy.wait()
-
-
-def pick(ids, full):
-    slabs, _, rows, lanes = full.shape
+def exchange_kernel(
+    groups, members, ids_ref, pieces_ref, items_ref, chosen, spread_send, spread_recv,
+    up_send, up_recv, down_send, down_recv, give_send, give_recv, local, *full
+):
+    chunks, _, blocks = pieces_ref.shape[:3]
+    wanted = items_ref.shape[2]
+    group = lax.axis_index("blk")
+    member = lax.axis_index("win")
+    mesh_id = pl.DeviceIdType.MESH
+
+    barrier = pltpu.get_barrier_semaphore()
+    for offset in range(1, groups):
+        pl.semaphore_signal(
+            barrier, inc=1, device_id=(lax.rem(group + offset, groups), member),
+            device_id_type=mesh_id,
+        )
+
+    @pl.when(member > 0)
+    def _():
+        pl.semaphore_signal(
+            barrier, inc=1, device_id=(group, member - 1), device_id_type=mesh_id
+        )
+
+    @pl.when(member < members - 1)
+    def _():
+        pl.semaphore_signal(
+            barrier, inc=1, device_id=(group, member + 1), device_id_type=mesh_id
+        )
+
+    beside = jnp.where(member > 0, 1, 0) + jnp.where(member < members - 1, 1, 0)
+    pl.semaphore_wait(barrier, groups - 1 + beside)
+
+    def spread(chunk, offset):
+        peer = lax.rem(group + offset, groups)
+        return pltpu.make_async_remote_copy(
+            src_ref=pieces_ref.at[chunk, peer],
+            dst_ref=full[chunk].at[member, pl.ds(group * blocks, blocks)],
+            send_sem=spread_send.at[chunk, offset],
+            recv_sem=spread_recv.at[chunk, offset],
+            device_id=(peer, member),
+            device_id_type=mesh_id,
+        )
+
+    def arrived(chunk, offset):
+        peer = lax.rem(group + groups - offset, groups)
+        here = full[chunk].at[member, pl.ds(peer * blocks, blocks)]
+        return pltpu.make_async_remote_copy(
+            src_ref=here,
+            dst_ref=here,
+            send_sem=spread_send.at[chunk, offset],
+            recv_sem=spread_recv.at[chunk, offset],
+            device_id=(peer, member),
+            device_id_type=mesh_id,
+        )
+
+    def kept(chunk):
+        return pltpu.make_async_copy(
+            pieces_ref.at[chunk, group],
+            full[chunk].at[member, pl.ds(group * blocks, blocks)],
+            local.at[0, chunk],
+        )
+
+    def up(chunk, step, slab):
+        return pltpu.make_async_remote_copy(
+            src_ref=full[chunk].at[slab],
+            dst_ref=full[chunk].at[slab],
+            send_sem=up_send.at[chunk, step],
+            recv_sem=up_recv.at[chunk, step],
+            device_id=(group, member + 1),
+            device_id_type=mesh_id,
+        )
+
+    def down(chunk, step, slab):
+        return pltpu.make_async_remote_copy(
+            src_ref=full[chunk].at[slab],
+            dst_ref=full[chunk].at[slab],
+            send_sem=down_send.at[chunk, step],
+            recv_sem=down_recv.at[chunk, step],
+            device_id=(group, member - 1),
+            device_id_type=mesh_id,
+        )
+
+    def forward(chunk, step, act):
+        @pl.when((member < members - 1) & (member >= step))
+        def _():
+            act(up(chunk, step, member - step))
+
+        @pl.when((member > 0) & (member + step <= members - 1))
+        def _():
+            act(down(chunk, step, member + step))
+
+    def receive(chunk, step):
+        @pl.when(member >= step + 1)
+        def _():
+            up(chunk, step, member - 1 - step).wait_recv()
+
+        @pl.when(member + 1 + step <= members - 1)
+        def _():
+            down(chunk, step, member + 1 + step).wait_recv()
+
+    def open_chunk(chunk):
+        kept(chunk).wait()
+        for offset in range(1, groups):
+            arrived(chunk, offset).wait_recv()
+        forward(chunk, 0, lambda copy: copy.start())
+
+    def give(chunk, offset):
+        peer = lax.rem(group + offset, groups)
+        return pltpu.make_async_remote_copy(
+            src_ref=chosen.at[chunk, offset],
+            dst_ref=items_ref.at[chunk, group],
+            send_sem=give_send.at[chunk, offset],
+            recv_sem=give_recv.at[chunk, offset],
+            device_id=(peer, member),
+            device_id_type=mesh_id,
+        )
+
+    def given(chunk, offset):
+        peer = lax.rem(group + groups - offset, groups)
+        return pltpu.make_async_remote_copy(
+            src_ref=chosen.at[chunk, offset],
+            dst_ref=items_ref.at[chunk, peer],
+            send_sem=give_send.at[chunk, offset],
+            recv_sem=give_recv.at[chunk, offset],
+            device_id=(peer, member),
+            device_id_type=mesh_id,
+        )
+
+    def mine(chunk):
+        return pltpu.make_async_copy(
+            chosen.at[chunk, 0], items_ref.at[chunk, group], local.at[1, chunk]
+        )
+
+    for chunk in range(chunks):
+        for offset in range(1, groups):
+            spread(chunk, offset).start()
+        kept(chunk).start()
+    open_chunk(0)
+    for chunk in range(chunks):
+        for step in range(1, members - 1):
+            receive(chunk, step - 1)
+            forward(chunk, step, lambda copy: copy.start())
+        if chunk + 1 < chunks:
+            open_chunk(chunk + 1)
+        receive(chunk, members - 2)
+        for offset in list(range(1, groups)) + [0]:
+            peer = lax.rem(group + offset, groups)
+            for slot in range(wanted):
+                chosen[chunk, offset, slot] = full[chunk][:, ids_ref[peer * wanted + slot]]
+            if offset:
+                give(chunk, offset).start()
+            else:
+                mine(chunk).start()
+    for chunk in range(chunks):
+        for step in range(members - 1):
+            forward(chunk, step, lambda copy: copy.wait_send())
+        for offset in range(1, groups):
+            spread(chunk, offset).wait_send()
+            give(chunk, offset).wait_send()
+            given(chunk, offset).wait_recv()
+        mine(chunk).wait()
+
+
+def exchange(ids, pieces, groups, members):
+    chunks, _, blocks, rows, lanes = pieces.shape
+    wanted = ids.shape[0] // groups
+    dma = pltpu.SemaphoreType.DMA
     return pl.pallas_call(
-        pick_kernel,
-        out_shape=jax.ShapeDtypeStruct((ids.shape[0], slabs, rows, lanes), full.dtype),
+        functools.partial(exchange_kernel, groups, members),
+        out_shape=jax.ShapeDtypeStruct(
+            (chunks, groups, wanted, members, rows, lanes), pieces.dtype
+        ),
         in_specs=[
             pl.BlockSpec(memory_space=pltpu.SMEM),
             pl.BlockSpec(memory_space=pl.ANY),
         ],
         out_specs=pl.BlockSpec(memory_space=pl.ANY),
-        scratch_shapes=[pltpu.SemaphoreType.DMA((ids.shape[0],))],
-    )(ids, full)
+        scratch_shapes=[
+            pltpu.VMEM((chunks, groups, wanted, members, rows, lanes), pieces.dtype),
+            dma((chunks, groups)),
+            dma((chunks, groups)),
+            dma((chunks, members)),
+            dma((chunks, members)),
+            dma((chunks, members)),
+            dma((chunks, members)),
+            dma((chunks, groups)),
+            dma((chunks, groups)),
+            dma((2, chunks)),
+        ]
+        + [
+            pltpu.VMEM((members, groups * blocks, rows, lanes), pieces.dtype)
+            for _ in range(chunks)
+        ],
+        compiler_params=pltpu.CompilerParams(
+            collective_id=0, has_side_effects=True, vmem_limit_bytes=32 * 2**20
+        ),
+    )(ids, pieces)
 
 
 def correlate_kernel(lane_parts, items_ref, lags_ref, out_ref, own, partners, even, odd):
-    pieces, blocks, slabs, rows, lanes = items_ref.shape
+    chunks, pieces, blocks, slabs, rows, chunk_lanes = items_ref.shape
     step = pl.program_id(0)
     pairs = blocks - 1
     depth = own.shape[1]
     block_rows = own.shape[0]
-    slab_lanes = lanes * lane_parts
+    parts_of_slab = lane_parts * chunks
 
     def shift(buffer, first):
         cosine, sine = lags_ref[0], lags_ref[1]
@@ -129,16 +305,18 @@
     @pl.when(step == 0)
     def _():
         for slab in range(slabs):
-            for lane in range(lane_parts):
-                at = slab * slab_lanes + lane * lanes
+            for place in range(parts_of_slab):
+                lane, chunk = place // chunks, place % chunks
+                at = (slab * parts_of_slab + place) * chunk_lanes
                 parts = range(lane, pieces, lane_parts)
-                mine = jnp.concatenate([items_ref[part, 0, slab] for part in parts], axis=0)
-                own[:, at : at + lanes] = mine.astype(jnp.float32)
+                mine = jnp.concatenate([items_ref[chunk, part, 0, slab] for part in parts], axis=0)
+                own[:, at : at + chunk_lanes] = mine.astype(jnp.float32)
                 for pair in range(pairs):
                     other = jnp.concatenate(
-                        [items_ref[part, 1 + pair, slab] for part in parts], axis=0
+                        [items_ref[chunk, part, 1 + pair, slab] for part in parts], axis=0
                     )
-                    partners[at : at + lanes, pair * block_rows : (pair + 1) * block_rows] = other.T
+                    columns = slice(pair * block_rows, (pair + 1) * block_rows)
+                    partners[at : at + chunk_lanes, columns] = other.T
         shift(even, 0)
 
     first = step * 2 * TILE
@@ -149,9 +327,9 @@
 
 
 def correlate(items, block_rows, lane_parts):
-    pieces, blocks, slabs, rows, lanes = items.shape
+    chunks, _, blocks, slabs, _, chunk_lanes = items.shape
     pairs = blocks - 1
-    depth = slabs * lanes * lane_parts
+    depth = slabs * chunks * chunk_lanes * lane_parts
     windows = depth // (2 * BINS)
     scale = 1.0 / math.sqrt(windows * BINS)
     return pl.pallas_call(
@@ -189,20 +367,15 @@
     lane_parts = max(1, groups // row_parts)
     lanes = slab_lanes // lane_parts
     rows = block_rows * lane_parts // groups
-    all_blocks = groups * members
+    chunks = lanes // LANES
     decks = lax.dynamic_slice_in_dim(deck_ids, group_index * members, members, 0)
-    pieces = whiten(record, decks, groups, block_rows, rows, lanes)
-    held = lax.all_to_all(pieces, "blk", split_axis=0, concat_axis=0, tiled=True)
-    held = held.reshape(all_blocks, rows, lanes)
-    full = lax.all_gather(held, "win", axis=0)
+    pieces = whiten(record, decks, block_rows, (chunks, groups, members, rows, LANES))
     own_ids = jnp.arange(groups, dtype=jnp.int32) * members + member_index
     rows_here = lax.dynamic_index_in_dim(
         partners.reshape(groups, members, -1), member_index, 1, keepdims=False
     )
     ids = jnp.concatenate([own_ids[:, None], rows_here], axis=1)
-    chosen = pick(ids.reshape(-1), full)
-    chosen = chosen.reshape(groups, ids.shape[1], members, rows, lanes)
-    items = lax.all_to_all(chosen, "blk", split_axis=0, concat_axis=0, tiled=True)
+    items = exchange(ids.reshape(-1), pieces, groups, members)
     return correlate(items, block_rows, lane_parts)
 
 

time: 217 us -> 87.4 us (0.40)
  blocking collectives: 48.9 us -> 0 us
  waiting for transfers between devices: 45 us -> 0 us
  Pallas kernels: 104 us -> 82.2 us
  between operations: 13.4 us -> 0.03 us
    all_to_all x2 -> x0, blocking collectives: 48.9 us -> none  [the longest x1 35.4 us: shards(): lax.all_to_all(chosen, 'blk', split_axis=0, concat_axis=0, tiled=True)]
    all_gather x1 -> x0, waiting for transfers between devices: 45 us -> none  [shards(): full = lax.all_gather(held, 'win', axis=0)]
    pallas_call x1, Pallas kernels: 81.5 us -> 59.4 us  [exchange(): pl.pallas_call(functools.partial(exchange_kernel, groups, members), out_s...]
  transfers between devices with their start and end apart: 1 -> 0, of which waited for: 1 -> 0; matrix products, arithmetic and copies ran while one was open for 0% -> 0% of each run, Pallas kernels for 0% -> 0%
where the time goes in v3:
time: 87.4 us; the launch traced here: 87.1 us
  Pallas kernels  82.2 us (94%)
  local copies, waits for them, and re-layouts  4.89 us (6%)
    pallas_call x1, Pallas kernels, exchange(): pl.pallas_call(functools.partial(exchange_kernel, groups, members), out_s...  59.4 us
    pallas_call x1, Pallas kernels, correlate(): pl.pallas_call(functools.partial(correlate_kernel, lane_parts), grid=(blo...  21.6 us
    unnamed x6, local copies, waits for them, and re-layouts  3.02 us

profile of v3, /device:TPU:1, one launch (start us, length us, event | category | flops | bytes accessed | tf_op | source)
XLA Modules:
  0.0 87.1 jit_solution(12114670447024228114)
XLA Ops:
  0.0 0.7 dynamic_slice.8.deck_ref
  0.7 0.8 reshape.16
  1.5 0.2 dynamic-slice_reduce_fusion
  1.7 0.1 copy.7
  1.8 0.1 reshape.17.ids_ref
  1.9 0.0 copy-start
  1.9 1.2 %copy-done = bf16[512,1024]{1,0:T(8,128)(2,1)S(1)} copy-done((bf16[512,1024]{1,0:T(8,128)(2,1)S(1)}, bf16[512,1024]{1,0:T(8,128)(2,1)}, u32[]{:S(2)}) %copy-start) | copy-done | bytes 1048600
  3.1 0.0 copy-start.1
  3.1 0.9 %copy-done.1 = bf16[512,256]{1,0:T(8,128)(2,1)S(1)} copy-done((bf16[512,256]{1,0:T(8,128)(2,1)S(1)}, bf16[512,256]{1,0:T(8,128)(2,1)}, u32[]{:S(2)}) %copy-start.1) | copy-done | bytes 262168
  4.1 1.1 %shard_map.55.pieces_ref = bf16[4,8,4,16,128]{4,3,2,1,0:T(8,128)(2,1)S(1)} custom-call(s32[4]{0:T(128)S(1)} %dynamic_slice.8.deck_ref, bf16[512,1024]{1,0:T(8,128)(2,1)S(1)} %copy-done, bf16[512,256]{1,0:T(8,128)(2,1)S(1)} %copy-done.1), custom_call_target="tpu_custom_call" | custom-call | tf_op jit(solution)/shard_map/pallas_call | solution.py:61
  5.2 59.4 %shard_map.56.items_ref = bf16[4,8,5,4,16,128]{5,4,3,2,1,0:T(8,128)(2,1)S(1)} custom-call(s32[40]{0:T(128)S(1)} %reshape.17.ids_ref, bf16[4,8,4,16,128]{4,3,2,1,0:T(8,128)(2,1)S(1)} %shard_map.55.pieces_ref), custom_call_target="tpu_custom_call" | custom-call | tf_op jit(solution)/shard_map/pallas_call | solution.py:241
  64.6 0.0 copy-start.2
  64.6 0.8 copy-done.2
  65.5 21.6 %shard_map.57 = bf16[4,64,16384]{2,1,0:T(8,128)(2,1)} custom-call(bf16[4,8,5,4,16,128]{5,4,3,2,1,0:T(8,128)(2,1)S(1)} %shard_map.56.items_ref, f32[2,64,128]{2,1,0:T(8,128)S(1)} %copy-done.2), custom_call_target="tpu_custom_call" | custom-call | flops 17179869184 | bytes 8388608 | tf_op jit(solution)/shard_map/pallas_call | solution.py:335
  (2 shorter events, 0.0 us)
Async XLA Ops:
  1.9 1.2 %copy-start = (bf16[512,1024]{1,0:T(8,128)(2,1)S(1)}, bf16[512,1024]{1,0:T(8,128)(2,1)}, u32[]{:S(2)}) copy-start(bf16[512,1024]{1,0:T(8,128)(2,1)} %record_ref.1) | copy-start | bytes 3145732
  3.1 0.9 %copy-start.1 = (bf16[512,256]{1,0:T(8,128)(2,1)S(1)}, bf16[512,256]{1,0:T(8,128)(2,1)}, u32[]{:S(2)}) copy-start(bf16[512,256]{1,0:T(8,128)(2,1)} %constant.26.clone.table_ref) | copy-start | bytes 786436
  64.6 0.8 copy-start.2

commit v4 on v3

--- a/solution.py
+++ b/solution.py
@@ -210,11 +210,11 @@
         kept(chunk).start()
     open_chunk(0)
     for chunk in range(chunks):
+        if chunk + 1 < chunks:
+            open_chunk(chunk + 1)
         for step in range(1, members - 1):
             receive(chunk, step - 1)
             forward(chunk, step, lambda copy: copy.start())
-        if chunk + 1 < chunks:
-            open_chunk(chunk + 1)
         receive(chunk, members - 2)
         for offset in list(range(1, groups)) + [0]:
             peer = lax.rem(group + offset, groups)

time: 87.4 us -> 85.9 us (0.983)
  Pallas kernels: 82.2 us -> 80.7 us
    pallas_call x1, Pallas kernels: 59.4 us -> 58 us  [exchange(): pl.pallas_call(functools.partial(exchange_kernel, groups, members), out_s...]
where the time goes in v4:
time: 85.9 us; the launch traced here: 85.7 us
  Pallas kernels  80.7 us (94%)
  local copies, waits for them, and re-layouts  4.89 us (6%)
    pallas_call x1, Pallas kernels, exchange(): pl.pallas_call(functools.partial(exchange_kernel, groups, members), out_s...  58 us
    pallas_call x1, Pallas kernels, correlate(): pl.pallas_call(functools.partial(correlate_kernel, lane_parts), grid=(blo...  21.6 us
    unnamed x6, local copies, waits for them, and re-layouts  3.02 us

profile of v4, /device:TPU:1, one launch (start us, length us, event | category | flops | bytes accessed | tf_op | source)
XLA Modules:
  0.0 85.7 jit_solution(385679127226324565)
XLA Ops:
  0.0 0.7 dynamic_slice.8.deck_ref
  0.7 0.8 reshape.16
  1.5 0.2 dynamic-slice_reduce_fusion
  1.7 0.1 copy.7
  1.8 0.1 reshape.17.ids_ref
  1.9 0.0 copy-start
  1.9 1.2 %copy-done = bf16[512,1024]{1,0:T(8,128)(2,1)S(1)} copy-done((bf16[512,1024]{1,0:T(8,128)(2,1)S(1)}, bf16[512,1024]{1,0:T(8,128)(2,1)}, u32[]{:S(2)}) %copy-start) | copy-done | bytes 1048600
  3.1 0.0 copy-start.1
  3.1 0.9 %copy-done.1 = bf16[512,256]{1,0:T(8,128)(2,1)S(1)} copy-done((bf16[512,256]{1,0:T(8,128)(2,1)S(1)}, bf16[512,256]{1,0:T(8,128)(2,1)}, u32[]{:S(2)}) %copy-start.1) | copy-done | bytes 262168
  4.1 1.1 %shard_map.55.pieces_ref = bf16[4,8,4,16,128]{4,3,2,1,0:T(8,128)(2,1)S(1)} custom-call(s32[4]{0:T(128)S(1)} %dynamic_slice.8.deck_ref, bf16[512,1024]{1,0:T(8,128)(2,1)S(1)} %copy-done, bf16[512,256]{1,0:T(8,128)(2,1)S(1)} %copy-done.1), custom_call_target="tpu_custom_call" | custom-call | tf_op jit(solution)/shard_map/pallas_call | solution.py:61
  5.2 58.0 %shard_map.56.items_ref = bf16[4,8,5,4,16,128]{5,4,3,2,1,0:T(8,128)(2,1)S(1)} custom-call(s32[40]{0:T(128)S(1)} %reshape.17.ids_ref, bf16[4,8,4,16,128]{4,3,2,1,0:T(8,128)(2,1)S(1)} %shard_map.55.pieces_ref), custom_call_target="tpu_custom_call" | custom-call | tf_op jit(solution)/shard_map/pallas_call | solution.py:241
  63.2 0.0 copy-start.2
  63.2 0.8 copy-done.2
  64.1 21.6 %shard_map.57 = bf16[4,64,16384]{2,1,0:T(8,128)(2,1)} custom-call(bf16[4,8,5,4,16,128]{5,4,3,2,1,0:T(8,128)(2,1)S(1)} %shard_map.56.items_ref, f32[2,64,128]{2,1,0:T(8,128)S(1)} %copy-done.2), custom_call_target="tpu_custom_call" | custom-call | flops 17179869184 | bytes 8388608 | tf_op jit(solution)/shard_map/pallas_call | solution.py:335
  (2 shorter events, 0.0 us)
Async XLA Ops:
  1.9 1.2 %copy-start = (bf16[512,1024]{1,0:T(8,128)(2,1)S(1)}, bf16[512,1024]{1,0:T(8,128)(2,1)}, u32[]{:S(2)}) copy-start(bf16[512,1024]{1,0:T(8,128)(2,1)} %record_ref.1) | copy-start | bytes 3145732
  3.1 0.9 %copy-start.1 = (bf16[512,256]{1,0:T(8,128)(2,1)S(1)}, bf16[512,256]{1,0:T(8,128)(2,1)}, u32[]{:S(2)}) copy-start(bf16[512,256]{1,0:T(8,128)(2,1)} %constant.26.clone.table_ref) | copy-start | bytes 786436
  63.2 0.8 copy-start.2

commit v5 on v4

--- a/solution.py
+++ b/solution.py
@@ -14,21 +14,90 @@
 LAGS = 64
 PIECE_ROWS = 16
 LANES = 128
+HALF = 64
 TILE = 8
+
+
+def halves(real, imag):
+    return np.concatenate([real[:, :HALF], imag[:, :HALF], real[:, HALF:], imag[:, HALF:]], axis=1)
 
 
 def forward_table():
     phases = np.arange(WS)[:, None] * np.arange(1, BINS + 1)[None, :] % WS
     angles = phases * (2.0 * math.pi / WS)
-    return jnp.asarray(np.concatenate([np.cos(angles), -np.sin(angles)], axis=1), jnp.bfloat16)
-
-
-def lag_table(scale):
+    return jnp.asarray(halves(np.cos(angles), -np.sin(angles)), jnp.bfloat16)
+
+
+def lag_table(windows):
     shifts = np.arange(LAGS) - LAGS // 2
     phases = shifts[:, None] * np.arange(1, BINS + 1)[None, :] % WS
     angles = phases * (2.0 * math.pi / WS)
-    table = np.stack([np.cos(angles), -np.sin(angles)], axis=0)
-    return jnp.asarray(table, jnp.bfloat16).astype(jnp.float32) * scale
+    cosine, sine = np.cos(angles), -np.sin(angles)
+    table = np.stack([halves(cosine, cosine), halves(sine, -sine)])
+    table = jnp.asarray(table, jnp.bfloat16).astype(jnp.float32)
+    return table / math.sqrt(windows * BINS)
+
+
+class Product:
+    def __init__(self, lane_parts, first_chunk, items, lags, own, turned, partners, even, odd):
+        self.lane_parts, self.first_chunk, self.items, self.lags = lane_parts, first_chunk, items, lags
+        self.own, self.turned, self.partners = own, turned, partners
+        self.even, self.odd = even, odd
+        chunks, _, _, slabs, _, _ = items.shape
+        self.places = [
+            (chunk, slab, lane)
+            for chunk in range(chunks)
+            for slab in range(slabs)
+            for lane in range(lane_parts)
+        ]
+
+    def load(self):
+        block_rows = self.own.shape[0]
+        pieces, blocks = self.items.shape[1:3]
+        for place, (chunk, slab, lane) in enumerate(self.places):
+            here = slice(place * LANES, (place + 1) * LANES)
+            parts = range(lane, pieces, self.lane_parts)
+
+            def gathered(slot):
+                return jnp.concatenate([self.items[chunk, part, slot, slab] for part in parts], axis=0)
+
+            mine = gathered(0).astype(jnp.float32)
+            self.own[:, here] = mine
+            self.turned[:, here] = jnp.concatenate([mine[:, HALF:], mine[:, :HALF]], axis=1)
+            for pair in range(blocks - 1):
+                self.partners[here, pair * block_rows : (pair + 1) * block_rows] = gathered(1 + pair).T
+
+    def shift(self, buffer, first):
+        for row in range(TILE):
+            line = self.own[pl.ds(first + row, 1), :]
+            turned = self.turned[pl.ds(first + row, 1), :]
+            for place, (chunk, _, _) in enumerate(self.places):
+                here = slice(place * LANES, (place + 1) * LANES)
+                half = (self.first_chunk + chunk) % 2
+                there = slice(half * LANES, (half + 1) * LANES)
+                buffer[row * LAGS : (row + 1) * LAGS, here] = (
+                    line[:, here] * self.lags[0, :, there] + turned[:, here] * self.lags[1, :, there]
+                ).astype(jnp.bfloat16)
+
+    def unit(self, step, emit):
+        first = step * 2 * TILE
+        self.shift(self.odd, first + TILE)
+        emit(0, self.multiply(self.even))
+        self.shift(self.even, lax.rem(first + 2 * TILE, self.own.shape[0]))
+        emit(1, self.multiply(self.odd))
+
+    def multiply(self, buffer):
+        return jnp.dot(buffer[...], self.partners[...], preferred_element_type=jnp.float32)
+
+
+def product_scratch(block_rows, depth, pairs):
+    return [
+        pltpu.VMEM((block_rows, depth), jnp.float32),
+        pltpu.VMEM((block_rows, depth), jnp.float32),
+        pltpu.VMEM((depth, pairs * block_rows), jnp.bfloat16),
+        pltpu.VMEM((TILE * LAGS, depth), jnp.bfloat16),
+        pltpu.VMEM((TILE * LAGS, depth), jnp.bfloat16),
+    ]
 
 
 def whiten_kernel(block_rows, deck_ref, record_ref, table_ref, out_ref):
@@ -72,11 +141,15 @@
 
 
 def exchange_kernel(
-    groups, members, ids_ref, pieces_ref, items_ref, chosen, spread_send, spread_recv,
-    up_send, up_recv, down_send, down_recv, give_send, give_recv, local, *full
+    groups, members, lane_parts, ids_ref, pieces_ref, lags_ref, items_ref, partial_ref, chosen,
+    spread_send, spread_recv, up_send, up_recv, down_send, down_recv, give_send, give_recv, local,
+    near, stage, stage_sems, own, turned, partners, even, odd, *full
 ):
     chunks, _, blocks = pieces_ref.shape[:3]
     wanted = items_ref.shape[2]
+    early = near.shape[0]
+    units = stage.shape[0]
+    product = Product(lane_parts, 0, near, lags_ref, own, turned, partners, even, odd)
     group = lax.axis_index("blk")
     member = lax.axis_index("win")
     mesh_id = pl.DeviceIdType.MESH
@@ -177,11 +250,14 @@
             arrived(chunk, offset).wait_recv()
         forward(chunk, 0, lambda copy: copy.start())
 
+    def landing(chunk, source):
+        return near.at[chunk, source] if chunk < early else items_ref.at[chunk - early, source]
+
     def give(chunk, offset):
         peer = lax.rem(group + offset, groups)
         return pltpu.make_async_remote_copy(
             src_ref=chosen.at[chunk, offset],
-            dst_ref=items_ref.at[chunk, group],
+            dst_ref=landing(chunk, group),
             send_sem=give_send.at[chunk, offset],
             recv_sem=give_recv.at[chunk, offset],
             device_id=(peer, member),
@@ -192,7 +268,7 @@
         peer = lax.rem(group + groups - offset, groups)
         return pltpu.make_async_remote_copy(
             src_ref=chosen.at[chunk, offset],
-            dst_ref=items_ref.at[chunk, peer],
+            dst_ref=landing(chunk, peer),
             send_sem=give_send.at[chunk, offset],
             recv_sem=give_recv.at[chunk, offset],
             device_id=(peer, member),
@@ -201,8 +277,24 @@
 
     def mine(chunk):
         return pltpu.make_async_copy(
-            chosen.at[chunk, 0], items_ref.at[chunk, group], local.at[1, chunk]
-        )
+            chosen.at[chunk, 0], landing(chunk, group), local.at[1, chunk]
+        )
+
+    def settle(chunk):
+        for offset in range(1, groups):
+            given(chunk, offset).wait_recv()
+        mine(chunk).wait()
+
+    def stored(step):
+        return pltpu.make_async_copy(stage.at[step], partial_ref.at[step], stage_sems.at[step])
+
+    def work(step, carry):
+        def emit(side, total):
+            stage[step, side * TILE * LAGS : (side + 1) * TILE * LAGS, :] = total
+
+        product.unit(step, emit)
+        stored(step).start()
+        return carry
 
     for chunk in range(chunks):
         for offset in range(1, groups):
@@ -212,10 +304,17 @@
     for chunk in range(chunks):
         if chunk + 1 < chunks:
             open_chunk(chunk + 1)
-        for step in range(1, members - 1):
-            receive(chunk, step - 1)
-            forward(chunk, step, lambda copy: copy.start())
-        receive(chunk, members - 2)
+        for step in range(members - 1):
+            if chunk == chunks - 1:
+                if step == 0:
+                    for before in range(early):
+                        settle(before)
+                    product.load()
+                    product.shift(even, 0)
+                work(step, 0)
+            receive(chunk, step)
+            if step + 1 < members - 1:
+                forward(chunk, step + 1, lambda copy: copy.start())
         for offset in list(range(1, groups)) + [0]:
             peer = lax.rem(group + offset, groups)
             for slot in range(wanted):
@@ -224,30 +323,41 @@
                 give(chunk, offset).start()
             else:
                 mine(chunk).start()
+    lax.fori_loop(members - 1, units, work, 0)
     for chunk in range(chunks):
         for step in range(members - 1):
             forward(chunk, step, lambda copy: copy.wait_send())
         for offset in range(1, groups):
             spread(chunk, offset).wait_send()
             give(chunk, offset).wait_send()
-            given(chunk, offset).wait_recv()
-        mine(chunk).wait()
-
-
-def exchange(ids, pieces, groups, members):
+        if chunk >= early:
+            settle(chunk)
+    for step in range(units):
+        stored(step).wait()
+
+
+def exchange(ids, pieces, lags, groups, members, block_rows, lane_parts):
     chunks, _, blocks, rows, lanes = pieces.shape
     wanted = ids.shape[0] // groups
+    early = chunks // 2
+    depth = early * members * lane_parts * lanes
+    columns = (wanted - 1) * block_rows
+    units = block_rows // (2 * TILE)
     dma = pltpu.SemaphoreType.DMA
     return pl.pallas_call(
-        functools.partial(exchange_kernel, groups, members),
-        out_shape=jax.ShapeDtypeStruct(
-            (chunks, groups, wanted, members, rows, lanes), pieces.dtype
+        functools.partial(exchange_kernel, groups, members, lane_parts),
+        out_shape=(
+            jax.ShapeDtypeStruct(
+                (chunks - early, groups, wanted, members, rows, lanes), pieces.dtype
+            ),
+            jax.ShapeDtypeStruct((units, 2 * TILE * LAGS, columns), jnp.float32),
         ),
         in_specs=[
             pl.BlockSpec(memory_space=pltpu.SMEM),
             pl.BlockSpec(memory_space=pl.ANY),
+            pl.BlockSpec(memory_space=pltpu.VMEM),
         ],
-        out_specs=pl.BlockSpec(memory_space=pl.ANY),
+        out_specs=(pl.BlockSpec(memory_space=pl.ANY), pl.BlockSpec(memory_space=pl.ANY)),
         scratch_shapes=[
             pltpu.VMEM((chunks, groups, wanted, members, rows, lanes), pieces.dtype),
             dma((chunks, groups)),
@@ -259,101 +369,69 @@
             dma((chunks, groups)),
             dma((chunks, groups)),
             dma((2, chunks)),
+            pltpu.VMEM((early, groups, wanted, members, rows, lanes), pieces.dtype),
+            pltpu.VMEM((units, 2 * TILE * LAGS, columns), jnp.float32),
+            dma((units,)),
         ]
+        + product_scratch(block_rows, depth, wanted - 1)
         + [
             pltpu.VMEM((members, groups * blocks, rows, lanes), pieces.dtype)
             for _ in range(chunks)
         ],
         compiler_params=pltpu.CompilerParams(
-            collective_id=0, has_side_effects=True, vmem_limit_bytes=32 * 2**20
+            collective_id=0, has_side_effects=True, vmem_limit_bytes=56 * 2**20
         ),
-    )(ids, pieces)
-
-
-def correlate_kernel(lane_parts, items_ref, lags_ref, out_ref, own, partners, even, odd):
-    chunks, pieces, blocks, slabs, rows, chunk_lanes = items_ref.shape
+    )(ids, pieces, lags)
+
+
+def correlate_kernel(
+    lane_parts, early, items_ref, lags_ref, partial_ref, out_ref, own, turned, partners, even, odd
+):
     step = pl.program_id(0)
-    pairs = blocks - 1
-    depth = own.shape[1]
-    block_rows = own.shape[0]
-    parts_of_slab = lane_parts * chunks
-
-    def shift(buffer, first):
-        cosine, sine = lags_ref[0], lags_ref[1]
-        for row in range(TILE):
-            line = own[pl.ds(first + row, 1), :]
-            for window in range(depth // (2 * BINS)):
-                base = window * 2 * BINS
-                real = line[:, base : base + BINS]
-                imag = line[:, base + BINS : base + 2 * BINS]
-                buffer[row * LAGS : (row + 1) * LAGS, base : base + BINS] = (
-                    real * cosine + imag * sine
-                ).astype(jnp.bfloat16)
-                buffer[row * LAGS : (row + 1) * LAGS, base + BINS : base + 2 * BINS] = (
-                    imag * cosine - real * sine
-                ).astype(jnp.bfloat16)
-
-    def multiply(buffer, first):
-        total = jnp.dot(buffer[...], partners[...], preferred_element_type=jnp.float32)
+    product = Product(lane_parts, early, items_ref, lags_ref, own, turned, partners, even, odd)
+    pairs, block_rows = out_ref.shape[0], own.shape[0]
+
+    @pl.when(step == 0)
+    def _():
+        product.load()
+        product.shift(even, 0)
+
+    def emit(side, total):
+        base = side * TILE
+        total = total + partial_ref[0, base * LAGS : (base + TILE) * LAGS, :]
         total = total.astype(jnp.bfloat16)
         for row in range(TILE):
+            at = (base + row) * block_rows
             for pair in range(pairs):
-                out_ref[pair, :, (first + row) * block_rows : (first + row + 1) * block_rows] = (
-                    total[row * LAGS : (row + 1) * LAGS, pair * block_rows : (pair + 1) * block_rows]
-                )
-
-    @pl.when(step == 0)
-    def _():
-        for slab in range(slabs):
-            for place in range(parts_of_slab):
-                lane, chunk = place // chunks, place % chunks
-                at = (slab * parts_of_slab + place) * chunk_lanes
-                parts = range(lane, pieces, lane_parts)
-                mine = jnp.concatenate([items_ref[chunk, part, 0, slab] for part in parts], axis=0)
-                own[:, at : at + chunk_lanes] = mine.astype(jnp.float32)
-                for pair in range(pairs):
-                    other = jnp.concatenate(
-                        [items_ref[chunk, part, 1 + pair, slab] for part in parts], axis=0
-                    )
-                    columns = slice(pair * block_rows, (pair + 1) * block_rows)
-                    partners[at : at + chunk_lanes, columns] = other.T
-        shift(even, 0)
-
-    first = step * 2 * TILE
-    shift(odd, first + TILE)
-    multiply(even, 0)
-    shift(even, lax.rem(first + 2 * TILE, block_rows))
-    multiply(odd, TILE)
-
-
-def correlate(items, block_rows, lane_parts):
+                out_ref[pair, :, at : at + block_rows] = total[
+                    row * LAGS : (row + 1) * LAGS, pair * block_rows : (pair + 1) * block_rows
+                ]
+
+    product.unit(step, emit)
+
+
+def correlate(items, lags, partial, block_rows, lane_parts, early):
     chunks, _, blocks, slabs, _, chunk_lanes = items.shape
     pairs = blocks - 1
     depth = slabs * chunks * chunk_lanes * lane_parts
-    windows = depth // (2 * BINS)
-    scale = 1.0 / math.sqrt(windows * BINS)
     return pl.pallas_call(
-        functools.partial(correlate_kernel, lane_parts),
+        functools.partial(correlate_kernel, lane_parts, early),
         grid=(block_rows // (2 * TILE),),
         out_shape=jax.ShapeDtypeStruct((pairs, LAGS, block_rows * block_rows), jnp.bfloat16),
         in_specs=[
             pl.BlockSpec(memory_space=pltpu.VMEM),
             pl.BlockSpec(memory_space=pltpu.VMEM),
+            pl.BlockSpec((1,) + partial.shape[1:], lambda i: (i, 0, 0)),
         ],
         out_specs=pl.BlockSpec((pairs, LAGS, 2 * TILE * block_rows), lambda i: (0, 0, i)),
-        scratch_shapes=[
-            pltpu.VMEM((block_rows, depth), jnp.float32),
-            pltpu.VMEM((depth, pairs * block_rows), jnp.bfloat16),
-            pltpu.VMEM((TILE * LAGS, depth), jnp.bfloat16),
-            pltpu.VMEM((TILE * LAGS, depth), jnp.bfloat16),
-        ],
+        scratch_shapes=product_scratch(block_rows, depth, pairs),
         compiler_params=pltpu.CompilerParams(vmem_limit_bytes=48 * 2**20),
         cost_estimate=pl.CostEstimate(
             flops=2 * LAGS * block_rows * depth * pairs * block_rows,
             bytes_accessed=pairs * LAGS * block_rows * block_rows * 2,
             transcendentals=0,
         ),
-    )(items, lag_table(scale))
+    )(items, lags, partial)
 
 
 def shards(record, deck_ids, partners):
@@ -375,8 +453,11 @@
         partners.reshape(groups, members, -1), member_index, 1, keepdims=False
     )
     ids = jnp.concatenate([own_ids[:, None], rows_here], axis=1)
-    items = exchange(ids.reshape(-1), pieces, groups, members)
-    return correlate(items, block_rows, lane_parts)
+    lags = lag_table(record.shape[1] // WS * members)
+    items, partial = exchange(
+        ids.reshape(-1), pieces, lags, groups, members, block_rows, lane_parts
+    )
+    return correlate(items, lags, partial, block_rows, lane_parts, chunks // 2)
 
 
 def solution(mesh):

time: 85.9 us -> 84.5 us (0.984)
  Pallas kernels: 80.7 us -> 76.3 us
  local copies, waits for them, and re-layouts: 4.89 us -> 7.63 us
    pallas_call x2, Pallas kernels: 79.6 us -> 75.1 us  [the longest x1 58.8 us: exchange(): pl.pallas_call(functools.partial(exchange_kernel, groups, members, lane_p...]
    unnamed x6 -> x10, local copies, waits for them, and re-layouts: 3.02 us -> 5.18 us
where the time goes in v5:
time: 84.5 us; the launch traced here: 83.9 us
  Pallas kernels  76.3 us (90%)
  local copies, waits for them, and re-layouts  7.63 us (9%)
    pallas_call x1, Pallas kernels, exchange(): pl.pallas_call(functools.partial(exchange_kernel, groups, members, lane_p...  58.8 us
    pallas_call x1, Pallas kernels, correlate(): pl.pallas_call(functools.partial(correlate_kernel, lane_parts, early), gr...  16.3 us
    unnamed x10, local copies, waits for them, and re-layouts  5.18 us

profile of v5, /device:TPU:1, one launch (start us, length us, event | category | flops | bytes accessed | tf_op | source)
XLA Modules:
  0.0 83.9 jit_solution(12983172011061468936)
XLA Ops:
  0.0 0.7 dynamic_slice.8.deck_ref
  0.7 0.8 reshape.16
  1.5 0.2 dynamic-slice_reduce_fusion
  1.7 0.1 copy.7
  1.8 0.7 reshape.17.ids_ref
  2.5 0.0 copy-start.1
  2.5 1.2 %copy-done.1 = bf16[512,1024]{1,0:T(8,128)(2,1)S(1)} copy-done((bf16[512,1024]{1,0:T(8,128)(2,1)S(1)}, bf16[512,1024]{1,0:T(8,128)(2,1)}, u32[]{:S(2)}) %copy-start.1) | copy-done | bytes 1048600
  3.7 0.0 copy-start.2
  3.7 0.9 %copy-done.2 = bf16[512,256]{1,0:T(8,128)(2,1)S(1)} copy-done((bf16[512,256]{1,0:T(8,128)(2,1)S(1)}, bf16[512,256]{1,0:T(8,128)(2,1)}, u32[]{:S(2)}) %copy-start.2) | copy-done | bytes 262168
  4.7 1.1 %shard_map.55.pieces_ref = bf16[4,8,4,16,128]{4,3,2,1,0:T(8,128)(2,1)S(1)} custom-call(s32[4]{0:T(128)S(1)} %dynamic_slice.8.deck_ref, bf16[512,1024]{1,0:T(8,128)(2,1)S(1)} %copy-done.1, bf16[512,256]{1,0:T(8,128)(2,1)S(1)} %copy-done.2), custom_call_target="tpu_custom_call" | custom-call | tf_op jit(solution)/shard_map/pallas_call | solution.py:130
  5.8 0.0 copy-start
  5.8 0.8 copy-done
  6.6 58.8 %shard_map.56 = (bf16[2,8,5,4,16,128]{5,4,3,2,1,0:T(8,128)(2,1)}, f32[8,1024,512]{2,1,0:T(8,128)}) custom-call(s32[40]{0:T(128)} %reshape.17.ids_ref, bf16[4,8,4,16,128]{4,3,2,1,0:T(8,128)(2,1)} %copy-done, f32[2,64,256]{2,1,0:T(8,128)} %constant.30.lags_ref), custom_call_target="tpu_custom_call" | custom-call | tf_op jit(solution)/shard_map/pallas_call | solution.py:347
  65.4 0.0 copy-start.3
  65.4 0.9 %copy-done.3 = f32[2,64,256]{2,1,0:T(8,128)S(1)} copy-done((f32[2,64,256]{2,1,0:T(8,128)S(1)}, f32[2,64,256]{2,1,0:T(8,128)}, u32[]{:S(2)}) %copy-start.3) | copy-done | bytes 131096
  66.3 0.0 copy-start.4
  66.3 1.3 %copy-done.4 = bf16[2,8,5,4,16,128]{5,4,3,2,1,0:T(8,128)(2,1)S(1)} copy-done((bf16[2,8,5,4,16,128]{5,4,3,2,1,0:T(8,128)(2,1)S(1)}, bf16[2,8,5,4,16,128]{5,4,3,2,1,0:T(8,128)(2,1)}, u32[]{:S(2)}) %copy-start.4) | copy-done | bytes 1310744
  67.6 16.3 %shard_map.57 = bf16[4,64,16384]{2,1,0:T(8,128)(2,1)} custom-call(bf16[2,8,5,4,16,128]{5,4,3,2,1,0:T(8,128)(2,1)S(1)} %copy-done.4, f32[2,64,256]{2,1,0:T(8,128)S(1)} %copy-done.3, f32[8,1024,512]{2,1,0:T(8,128)} %get-tuple-element.8.partial_ref), custom_call_target="tpu_custom_call" | custom-call | flops 8589934592 | bytes 8388608 | tf_op jit(solution)/shard_map/pallas_call | solution.py:417
  (2 shorter events, 0.0 us)
Async XLA Ops:
  2.5 1.2 %copy-start.1 = (bf16[512,1024]{1,0:T(8,128)(2,1)S(1)}, bf16[512,1024]{1,0:T(8,128)(2,1)}, u32[]{:S(2)}) copy-start(bf16[512,1024]{1,0:T(8,128)(2,1)} %record_ref.1) | copy-start | bytes 3145732
  3.7 0.9 %copy-start.2 = (bf16[512,256]{1,0:T(8,128)(2,1)S(1)}, bf16[512,256]{1,0:T(8,128)(2,1)}, u32[]{:S(2)}) copy-start(bf16[512,256]{1,0:T(8,128)(2,1)} %constant.27.clone.table_ref) | copy-start | bytes 786436
  5.8 0.8 copy-start
  65.4 0.9 %copy-start.3 = (f32[2,64,256]{2,1,0:T(8,128)S(1)}, f32[2,64,256]{2,1,0:T(8,128)}, u32[]{:S(2)}) copy-start(f32[2,64,256]{2,1,0:T(8,128)} %constant.30.lags_ref) | copy-start | bytes 393220
  66.3 1.3 %copy-start.4 = (bf16[2,8,5,4,16,128]{5,4,3,2,1,0:T(8,128)(2,1)S(1)}, bf16[2,8,5,4,16,128]{5,4,3,2,1,0:T(8,128)(2,1)}, u32[]{:S(2)}) copy-start(bf16[2,8,5,4,16,128]{5,4,3,2,1,0:T(8,128)(2,1)} %get-tuple-element.7.items_ref) | copy-start | bytes 3932164

commit v6 on v5

--- a/solution.py
+++ b/solution.py
@@ -102,11 +102,12 @@
 
 def whiten_kernel(block_rows, deck_ref, record_ref, table_ref, out_ref):
     chunks, pieces, blocks, rows, chunk_lanes = out_ref.shape
+    first_block = lax.axis_index("blk") * blocks
     windows = record_ref.shape[1] // WS
     lane_parts = windows * 2 * BINS // (chunks * chunk_lanes)
     for block in range(blocks):
         here = pl.ds(block * block_rows, block_rows)
-        polarity = (1 - 2 * deck_ref[block]).astype(jnp.float32)
+        polarity = (1 - 2 * deck_ref[first_block + block]).astype(jnp.float32)
         values = []
         for window in range(windows):
             spectra = jnp.dot(
@@ -141,7 +142,7 @@
 
 
 def exchange_kernel(
-    groups, members, lane_parts, ids_ref, pieces_ref, lags_ref, items_ref, partial_ref, chosen,
+    groups, members, lane_parts, partners_ref, pieces_ref, lags_ref, items_ref, partial_ref, chosen,
     spread_send, spread_recv, up_send, up_recv, down_send, down_recv, give_send, give_recv, local,
     near, stage, stage_sems, own, turned, partners, even, odd, *full
 ):
@@ -318,7 +319,10 @@
         for offset in list(range(1, groups)) + [0]:
             peer = lax.rem(group + offset, groups)
             for slot in range(wanted):
-                chosen[chunk, offset, slot] = full[chunk][:, ids_ref[peer * wanted + slot]]
+                item = peer * members + member
+                if slot:
+                    item = partners_ref[item, slot - 1]
+                chosen[chunk, offset, slot] = full[chunk][:, item]
             if offset:
                 give(chunk, offset).start()
             else:
@@ -336,9 +340,9 @@
         stored(step).wait()
 
 
-def exchange(ids, pieces, lags, groups, members, block_rows, lane_parts):
+def exchange(listed, pieces, lags, groups, members, block_rows, lane_parts):
     chunks, _, blocks, rows, lanes = pieces.shape
-    wanted = ids.shape[0] // groups
+    wanted = 1 + listed.shape[1]
     early = chunks // 2
     depth = early * members * lane_parts * lanes
     columns = (wanted - 1) * block_rows
@@ -381,7 +385,7 @@
         compiler_params=pltpu.CompilerParams(
             collective_id=0, has_side_effects=True, vmem_limit_bytes=56 * 2**20
         ),
-    )(ids, pieces, lags)
+    )(listed, pieces, lags)
 
 
 def correlate_kernel(
@@ -437,8 +441,6 @@
 def shards(record, deck_ids, partners):
     groups = lax.axis_size("blk")
     members = lax.axis_size("win")
-    group_index = lax.axis_index("blk")
-    member_index = lax.axis_index("win")
     block_rows = record.shape[0] // members
     slab_lanes = record.shape[1] // WS * 2 * BINS
     row_parts = block_rows // PIECE_ROWS
@@ -446,16 +448,10 @@
     lanes = slab_lanes // lane_parts
     rows = block_rows * lane_parts // groups
     chunks = lanes // LANES
-    decks = lax.dynamic_slice_in_dim(deck_ids, group_index * members, members, 0)
-    pieces = whiten(record, decks, block_rows, (chunks, groups, members, rows, LANES))
-    own_ids = jnp.arange(groups, dtype=jnp.int32) * members + member_index
-    rows_here = lax.dynamic_index_in_dim(
-        partners.reshape(groups, members, -1), member_index, 1, keepdims=False
-    )
-    ids = jnp.concatenate([own_ids[:, None], rows_here], axis=1)
+    pieces = whiten(record, deck_ids, block_rows, (chunks, groups, members, rows, LANES))
     lags = lag_table(record.shape[1] // WS * members)
     items, partial = exchange(
-        ids.reshape(-1), pieces, lags, groups, members, block_rows, lane_parts
+        partners, pieces, lags, groups, members, block_rows, lane_parts
     )
     return correlate(items, lags, partial, block_rows, lane_parts, chunks // 2)
 

time: 84.5 us -> 84.1 us (level)
    unnamed x10 -> x13, local copies, waits for them, and re-layouts: 5.18 us -> 7.19 us
    reshape x2 -> x0, local copies, waits for them, and re-layouts: 1.43 us -> none  [the longest x1 0.76 us: shards(): partners.reshape(groups, members, -1)]
    dynamic_slice x2 -> x0, local copies, waits for them, and re-layouts: 0.95 us -> none  [the longest x1 0.73 us: shards(): lax.dynamic_slice_in_dim(deck_ids, group_index * members, members, 0)]
where the time goes in v6:
time: 84.1 us; the launch traced here: 83.5 us
  Pallas kernels  76.3 us (91%)
  local copies, waits for them, and re-layouts  7.19 us (9%)
    pallas_call x1, Pallas kernels, exchange(): pl.pallas_call(functools.partial(exchange_kernel, groups, members, lane_p...  58.8 us
    pallas_call x1, Pallas kernels, correlate(): pl.pallas_call(functools.partial(correlate_kernel, lane_parts, early), gr...  16.4 us
    unnamed x13, local copies, waits for them, and re-layouts  7.19 us

profile of v6, /device:TPU:1, one launch (start us, length us, event | category | flops | bytes accessed | tf_op | source)
XLA Modules:
  0.0 83.5 jit_solution(8544604603676293594)
XLA Ops:
  0.0 1.4 %copy.6.partners_ref = s32[32,4]{1,0:T(8,128)} copy(s32[32,4]{0,1:T(4,128)} %param.7) | data formatting | bytes 1024 | tf_op args[2]
  1.4 0.0 copy-start.1
  1.4 1.2 %copy-done.1 = bf16[512,1024]{1,0:T(8,128)(2,1)S(1)} copy-done((bf16[512,1024]{1,0:T(8,128)(2,1)S(1)}, bf16[512,1024]{1,0:T(8,128)(2,1)}, u32[]{:S(2)}) %copy-start.1) | copy-done | bytes 1048600
  2.6 0.0 copy-start.2
  2.6 0.9 %copy-done.2 = bf16[512,256]{1,0:T(8,128)(2,1)S(1)} copy-done((bf16[512,256]{1,0:T(8,128)(2,1)S(1)}, bf16[512,256]{1,0:T(8,128)(2,1)}, u32[]{:S(2)}) %copy-start.2) | copy-done | bytes 262168
  3.5 0.0 copy-start.4
  3.5 0.7 copy-done.4
  4.2 1.1 %shard_map.55.pieces_ref = bf16[4,8,4,16,128]{4,3,2,1,0:T(8,128)(2,1)S(1)} custom-call(s32[32]{0:T(128)S(1)} %copy-done.4, bf16[512,1024]{1,0:T(8,128)(2,1)S(1)} %copy-done.1, bf16[512,256]{1,0:T(8,128)(2,1)S(1)} %copy-done.2), custom_call_target="tpu_custom_call" | custom-call | tf_op jit(solution)/shard_map/pallas_call | solution.py:131
  5.3 0.0 copy-start
  5.3 0.8 copy-done
  6.1 58.8 %shard_map.56 = (bf16[2,8,5,4,16,128]{5,4,3,2,1,0:T(8,128)(2,1)}, f32[8,1024,512]{2,1,0:T(8,128)}) custom-call(s32[32,4]{1,0:T(8,128)} %copy.6.partners_ref, bf16[4,8,4,16,128]{4,3,2,1,0:T(8,128)(2,1)} %copy-done, f32[2,64,256]{2,1,0:T(8,128)} %constant.10.lags_ref), custom_call_target="tpu_custom_call" | custom-call | tf_op jit(solution)/shard_map/pallas_call | solution.py:351
  64.9 0.0 copy-start.3
  64.9 0.9 %copy-done.3 = f32[2,64,256]{2,1,0:T(8,128)S(1)} copy-done((f32[2,64,256]{2,1,0:T(8,128)S(1)}, f32[2,64,256]{2,1,0:T(8,128)}, u32[]{:S(2)}) %copy-start.3) | copy-done | bytes 131096
  65.8 0.0 copy-start.5
  65.8 1.3 %copy-done.5 = bf16[2,8,5,4,16,128]{5,4,3,2,1,0:T(8,128)(2,1)S(1)} copy-done((bf16[2,8,5,4,16,128]{5,4,3,2,1,0:T(8,128)(2,1)S(1)}, bf16[2,8,5,4,16,128]{5,4,3,2,1,0:T(8,128)(2,1)}, u32[]{:S(2)}) %copy-start.5) | copy-done | bytes 1310744
  67.2 16.4 %shard_map.57 = bf16[4,64,16384]{2,1,0:T(8,128)(2,1)} custom-call(bf16[2,8,5,4,16,128]{5,4,3,2,1,0:T(8,128)(2,1)S(1)} %copy-done.5, f32[2,64,256]{2,1,0:T(8,128)S(1)} %copy-done.3, f32[8,1024,512]{2,1,0:T(8,128)} %get-tuple-element.8.partial_ref), custom_call_target="tpu_custom_call" | custom-call | flops 8589934592 | bytes 8388608 | tf_op jit(solution)/shard_map/pallas_call | solution.py:421
Async XLA Ops:
  1.4 1.2 %copy-start.1 = (bf16[512,1024]{1,0:T(8,128)(2,1)S(1)}, bf16[512,1024]{1,0:T(8,128)(2,1)}, u32[]{:S(2)}) copy-start(bf16[512,1024]{1,0:T(8,128)(2,1)} %record_ref.1) | copy-start | bytes 3145732
  2.6 0.9 %copy-start.2 = (bf16[512,256]{1,0:T(8,128)(2,1)S(1)}, bf16[512,256]{1,0:T(8,128)(2,1)}, u32[]{:S(2)}) copy-start(bf16[512,256]{1,0:T(8,128)(2,1)} %constant.7.clone.table_ref) | copy-start | bytes 786436
  3.5 0.7 copy-start.4
  5.3 0.8 copy-start
  64.9 0.9 %copy-start.3 = (f32[2,64,256]{2,1,0:T(8,128)S(1)}, f32[2,64,256]{2,1,0:T(8,128)}, u32[]{:S(2)}) copy-start(f32[2,64,256]{2,1,0:T(8,128)} %constant.10.lags_ref) | copy-start | bytes 393220
  65.8 1.3 %copy-start.5 = (bf16[2,8,5,4,16,128]{5,4,3,2,1,0:T(8,128)(2,1)S(1)}, bf16[2,8,5,4,16,128]{5,4,3,2,1,0:T(8,128)(2,1)}, u32[]{:S(2)}) copy-start(bf16[2,8,5,4,16,128]{5,4,3,2,1,0:T(8,128)(2,1)} %get-tuple-element.7.items_ref) | copy-start | bytes 3932164

commit v7 on v6

--- a/solution.py
+++ b/solution.py
@@ -306,16 +306,16 @@
         if chunk + 1 < chunks:
             open_chunk(chunk + 1)
         for step in range(members - 1):
-            if chunk == chunks - 1:
-                if step == 0:
-                    for before in range(early):
-                        settle(before)
-                    product.load()
-                    product.shift(even, 0)
-                work(step, 0)
             receive(chunk, step)
             if step + 1 < members - 1:
                 forward(chunk, step + 1, lambda copy: copy.start())
+            if chunk == chunks - 1 and step == 0:
+                for before in range(early):
+                    settle(before)
+                product.load()
+                product.shift(even, 0)
+            elif chunk == chunks - 1 and step + 1 < members - 1:
+                work(step - 1, 0)
         for offset in list(range(1, groups)) + [0]:
             peer = lax.rem(group + offset, groups)
             for slot in range(wanted):
@@ -327,7 +327,7 @@
                 give(chunk, offset).start()
             else:
                 mine(chunk).start()
-    lax.fori_loop(members - 1, units, work, 0)
+    lax.fori_loop(members - 3, units, work, 0)
     for chunk in range(chunks):
         for step in range(members - 1):
             forward(chunk, step, lambda copy: copy.wait_send())

time: 84.1 us -> 85 us (1.011)
  no operation moved by 1% of the time
where the time goes in v7:
time: 85 us; the launch traced here: 83.6 us
  Pallas kernels  76.3 us (90%)
  local copies, waits for them, and re-layouts  7.19 us (8%)
    pallas_call x1, Pallas kernels, exchange(): pl.pallas_call(functools.partial(exchange_kernel, groups, members, lane_p...  58.9 us
    pallas_call x1, Pallas kernels, correlate(): pl.pallas_call(functools.partial(correlate_kernel, lane_parts, early), gr...  16.4 us
    unnamed x13, local copies, waits for them, and re-layouts  7.19 us

profile of v7, /device:TPU:1, one launch (start us, length us, event | category | flops | bytes accessed | tf_op | source)
XLA Modules:
  0.0 83.6 jit_solution(3730261605535328048)
XLA Ops:
  0.0 1.4 %copy.6.partners_ref = s32[32,4]{1,0:T(8,128)} copy(s32[32,4]{0,1:T(4,128)} %param.7) | data formatting | bytes 1024 | tf_op args[2]
  1.4 0.0 copy-start.1
  1.4 1.2 %copy-done.1 = bf16[512,1024]{1,0:T(8,128)(2,1)S(1)} copy-done((bf16[512,1024]{1,0:T(8,128)(2,1)S(1)}, bf16[512,1024]{1,0:T(8,128)(2,1)}, u32[]{:S(2)}) %copy-start.1) | copy-done | bytes 1048600
  2.6 0.0 copy-start.2
  2.6 0.9 %copy-done.2 = bf16[512,256]{1,0:T(8,128)(2,1)S(1)} copy-done((bf16[512,256]{1,0:T(8,128)(2,1)S(1)}, bf16[512,256]{1,0:T(8,128)(2,1)}, u32[]{:S(2)}) %copy-start.2) | copy-done | bytes 262168
  3.5 0.0 copy-start.4
  3.5 0.7 copy-done.4
  4.2 1.1 %shard_map.55.pieces_ref = bf16[4,8,4,16,128]{4,3,2,1,0:T(8,128)(2,1)S(1)} custom-call(s32[32]{0:T(128)S(1)} %copy-done.4, bf16[512,1024]{1,0:T(8,128)(2,1)S(1)} %copy-done.1, bf16[512,256]{1,0:T(8,128)(2,1)S(1)} %copy-done.2), custom_call_target="tpu_custom_call" | custom-call | tf_op jit(solution)/shard_map/pallas_call | solution.py:131
  5.3 0.0 copy-start
  5.3 0.8 copy-done
  6.1 58.9 %shard_map.56 = (bf16[2,8,5,4,16,128]{5,4,3,2,1,0:T(8,128)(2,1)}, f32[8,1024,512]{2,1,0:T(8,128)}) custom-call(s32[32,4]{1,0:T(8,128)} %copy.6.partners_ref, bf16[4,8,4,16,128]{4,3,2,1,0:T(8,128)(2,1)} %copy-done, f32[2,64,256]{2,1,0:T(8,128)} %constant.10.lags_ref), custom_call_target="tpu_custom_call" | custom-call | tf_op jit(solution)/shard_map/pallas_call | solution.py:351
  65.0 0.0 copy-start.3
  65.0 0.9 %copy-done.3 = f32[2,64,256]{2,1,0:T(8,128)S(1)} copy-done((f32[2,64,256]{2,1,0:T(8,128)S(1)}, f32[2,64,256]{2,1,0:T(8,128)}, u32[]{:S(2)}) %copy-start.3) | copy-done | bytes 131096
  65.9 0.0 copy-start.5
  65.9 1.3 %copy-done.5 = bf16[2,8,5,4,16,128]{5,4,3,2,1,0:T(8,128)(2,1)S(1)} copy-done((bf16[2,8,5,4,16,128]{5,4,3,2,1,0:T(8,128)(2,1)S(1)}, bf16[2,8,5,4,16,128]{5,4,3,2,1,0:T(8,128)(2,1)}, u32[]{:S(2)}) %copy-start.5) | copy-done | bytes 1310744
  67.2 16.4 %shard_map.57 = bf16[4,64,16384]{2,1,0:T(8,128)(2,1)} custom-call(bf16[2,8,5,4,16,128]{5,4,3,2,1,0:T(8,128)(2,1)S(1)} %copy-done.5, f32[2,64,256]{2,1,0:T(8,128)S(1)} %copy-done.3, f32[8,1024,512]{2,1,0:T(8,128)} %get-tuple-element.8.partial_ref), custom_call_target="tpu_custom_call" | custom-call | flops 8589934592 | bytes 8388608 | tf_op jit(solution)/shard_map/pallas_call | solution.py:421
Async XLA Ops:
  1.4 1.2 %copy-start.1 = (bf16[512,1024]{1,0:T(8,128)(2,1)S(1)}, bf16[512,1024]{1,0:T(8,128)(2,1)}, u32[]{:S(2)}) copy-start(bf16[512,1024]{1,0:T(8,128)(2,1)} %record_ref.1) | copy-start | bytes 3145732
  2.6 0.9 %copy-start.2 = (bf16[512,256]{1,0:T(8,128)(2,1)S(1)}, bf16[512,256]{1,0:T(8,128)(2,1)}, u32[]{:S(2)}) copy-start(bf16[512,256]{1,0:T(8,128)(2,1)} %constant.7.clone.table_ref) | copy-start | bytes 786436
  3.5 0.7 copy-start.4
  5.3 0.8 copy-start
  65.0 0.9 %copy-start.3 = (f32[2,64,256]{2,1,0:T(8,128)S(1)}, f32[2,64,256]{2,1,0:T(8,128)}, u32[]{:S(2)}) copy-start(f32[2,64,256]{2,1,0:T(8,128)} %constant.10.lags_ref) | copy-start | bytes 393220
  65.9 1.3 %copy-start.5 = (bf16[2,8,5,4,16,128]{5,4,3,2,1,0:T(8,128)(2,1)S(1)}, bf16[2,8,5,4,16,128]{5,4,3,2,1,0:T(8,128)(2,1)}, u32[]{:S(2)}) copy-start(bf16[2,8,5,4,16,128]{5,4,3,2,1,0:T(8,128)(2,1)} %get-tuple-element.7.items_ref) | copy-start | bytes 3932164
